TPU v7x, 512 devices: a whole 4x8x8 slice. The times are simulated.
512 devices in a mesh: dp: 8 (over z), expert: 64 (over y, x, core).
Axes of the slice: x: 4, y: 8, z: 8, core: 2. Of those that a mesh axis runs over, the one named last changes fastest.
Arguments:
- tokens: bfloat16 [65536, 2048], P(('dp', 'expert')), may hold values from -24 to 24
- latent_grad: bfloat16 [65536, 512], P(('dp', 'expert')), may hold values from -6 to 6
- routes: int32 [65536, 8], P(('dp', 'expert')), may hold values from 0 to 63, all different within a row; in each aligned block of 128 rows (0 to 127, 128 to 255, ...) at most 24 rows name the same one
- route_weights: bfloat16 [65536, 8], P(('dp', 'expert')), may hold values from 0.099609375 to 1
- down_proj: bfloat16 [2048, 512], P(('dp', 'expert')), may hold values from -0.125 to 0.125
- expert_up: bfloat16 [64, 512, 1024], P('expert'), may hold values from -0.25 to 0.25
- expert_down: bfloat16 [64, 1024, 512], P('expert'), may hold values from -0.1875 to 0.1875
Outputs:
- input_grad: bfloat16 [65536, 2048], P(('dp', 'expert'))
- proj_grad: float32 [2048, 512], P(('dp', 'expert'))
- weight_grad: bfloat16 [65536, 8], P(('dp', 'expert'))
Inputs may be any that keep to these rules, and one draw needn't show every extreme that they name: `routes`: each row names 8 different experts. Within the rows of one device (aligned blocks of 128 rows) no expert is named by more than 24 rows, a bound that some block reaches; every expert is named somewhere.
All inputs are finite; a program needn't handle non-finite values.
Results may differ from a plain program's by a relative error of at most 0.009.
Values may be sent and summed in bfloat16 or wider, within the bound.
A program may use at most 64 MiB of HBM per device.

v0:
```python
import jax
import jax.numpy as jnp
from jax import lax
from jax.sharding import PartitionSpec as P


def on_device(tokens, latent_grad, routes, route_weights, down_proj, expert_up, expert_down):
    tok_rows = tokens.shape[0]
    top_k = routes.shape[1]
    lat_width = latent_grad.shape[1]
    experts = lax.axis_size("expert")
    capacity = 3 * tok_rows * top_k // (2 * experts)
    whole_proj = lax.all_gather(down_proj, ("dp", "expert"), axis=0, tiled=True)
    latent = jnp.dot(tokens, whole_proj, preferred_element_type=jnp.float32).astype(jnp.bfloat16)
    flat_ids = routes.reshape(-1)
    onehot = (flat_ids[:, None] == jnp.arange(experts, dtype=jnp.int32)[None, :]).astype(jnp.int32)
    before = jnp.cumsum(onehot, axis=0) - onehot
    position = jnp.sum(before * onehot, axis=1)
    slot_index = flat_ids * capacity + position
    owner_row = jnp.arange(tok_rows * top_k, dtype=jnp.int32) // top_k
    sent_latent = (
        jnp.zeros((experts * capacity, lat_width), jnp.bfloat16)
        .at[slot_index]
        .set(latent[owner_row])
    )
    sent_grad = (
        jnp.zeros((experts * capacity, lat_width), jnp.bfloat16)
        .at[slot_index]
        .set(latent_grad[owner_row])
    )
    sent_weight = (
        jnp.zeros((experts * capacity,), jnp.bfloat16).at[slot_index].set(route_weights.reshape(-1))
    )
    sent_latent = sent_latent.reshape(experts, capacity, lat_width)
    sent_grad = sent_grad.reshape(experts, capacity, lat_width)
    sent_weight = sent_weight.reshape(experts, capacity)
    up_matrix = expert_up[0]
    down_matrix = expert_down[0]
    got_latent = lax.all_to_all(sent_latent, "expert", split_axis=0, concat_axis=0, tiled=True)
    got_grad = lax.all_to_all(sent_grad, "expert", split_axis=0, concat_axis=0, tiled=True)
    got_weight = lax.all_to_all(sent_weight, "expert", split_axis=0, concat_axis=0, tiled=True)
    sources, count = got_weight.shape
    rows_latent = got_latent.reshape(sources * count, lat_width)
    rows_grad = got_grad.reshape(sources * count, lat_width)
    pre_act = jnp.dot(rows_latent, up_matrix, preferred_element_type=jnp.float32)
    back_grad = lax.dot_general(
        rows_grad, down_matrix, (((1,), (1,)), ((), ())), preferred_element_type=jnp.float32
    )
    active = jnp.maximum(pre_act, 0.0)
    weight_part = jnp.sum(back_grad * active * active, axis=1).astype(jnp.bfloat16)
    scales = got_weight.reshape(sources * count).astype(jnp.float32)
    pre_grad = (scales[:, None] * back_grad * (2.0 * active)).astype(jnp.bfloat16)
    row_grad = lax.dot_general(
        pre_grad, up_matrix, (((1,), (1,)), ((), ())), preferred_element_type=jnp.float32
    ).astype(jnp.bfloat16)
    back_rows = lax.all_to_all(
        row_grad.reshape(sources, count, lat_width),
        "expert",
        split_axis=0,
        concat_axis=0,
        tiled=True,
    )
    back_weights = lax.all_to_all(
        weight_part.reshape(sources, count), "expert", split_axis=0, concat_axis=0, tiled=True
    )
    rows_flat = back_rows.reshape(experts * capacity, lat_width)
    mine = rows_flat[slot_index].astype(jnp.float32).reshape(tok_rows, top_k, lat_width)
    latent_sum = jnp.sum(mine, axis=1).astype(jnp.bfloat16)
    weight_grad = back_weights.reshape(experts * capacity)[slot_index].reshape(tok_rows, top_k)
    input_grad = lax.dot_general(
        latent_sum, whole_proj, (((1,), (1,)), ((), ())), preferred_element_type=jnp.float32
    ).astype(jnp.bfloat16)
    proj_grad = lax.psum_scatter(
        lax.dot_general(
            tokens, latent_sum, (((0,), (0,)), ((), ())), preferred_element_type=jnp.float32
        ),
        ("dp", "expert"),
        scatter_dimension=0,
        tiled=True,
    )
    return (input_grad, proj_grad, weight_grad)


def solution(mesh):
    placed = (
        P(("dp", "expert"), None),
        P(("dp", "expert"), None),
        P(("dp", "expert"), None),
        P(("dp", "expert"), None),
        P(("dp", "expert"), None),
        P("expert", None, None),
        P("expert", None, None),
    )
    return jax.shard_map(
        on_device,
        mesh=mesh,
        in_specs=placed,
        out_specs=(P(("dp", "expert"), None), P(("dp", "expert"), None), P(("dp", "expert"), None)),
        check_vma=False,
    )
```

profile of v0, /device:TPU:1, one launch (start us, length us, event | category | flops | bytes accessed | tf_op | source)
XLA Modules:
  0.0 594.8 jit_solution(8026868387498040939)
XLA Ops:
  7.2 0.0 copy-start
  7.2 0.0 all-gather.3.cloned.1.call-start
  7.2 0.7 all-gather.3.cloned.1.call-update
  7.9 0.8 copy.20
  8.7 0.1 eq.29
  8.8 0.1 eq.25
  8.9 18.0 %reduce-window.6 = s32[64,8,128]{2,1,0:T(8,128)S(1)} reduce-window(s32[64,8,128]{2,1,0:T(8,128)S(1)} %fusion.20, s32[]{:T(128)} %constant.30.clone.1), window={size=1x1x128 pad=0_0x0_0x127_0}, to_apply=%region_0.0 | reduce-window | flops 8323072 | bytes 524292 | tf_op jit(solution)/shard_map/reduce-window
  26.9 0.1 slice.16
  27.1 0.1 copy.22
  27.2 0.1 copy.23
  27.3 0.7 broadcast_multiply_fusion
  28.0 0.1 copy.19
  28.1 0.1 mul.44
  28.2 0.8 copy.24
  29.0 0.1 reshape.200
  29.1 0.1 broadcast_add_fusion
  29.3 0.1 fusion.19
  29.4 7.6 %scatter_custom_fusion = bf16[1536]{0:T(1024)(128)(2,1)S(1)} fusion(s32[1024]{0:T(1024)S(1)} %bitcast.61, bf16[1024]{0:T(1024)(128)(2,1)S(1)} %reshape.200, bf16[]{:T(256)} %constant.28.clone.1), kind=kCustom, calls=%fused_computation.48 | custom fusion | bytes 3074 | tf_op jit(solution)/shard_map/scatter | solution.py:32
  37.0 0.7 all_to_all.25
  37.7 11.6 %all-to-all-start = ((bf16[64,1,24]{2,1,0:T(2,128)(2,1)}), bf16[64,1,24]{2,1,0:T(2,128)(2,1)S(1)}, u32[]{:S(2)}, u32[]{:S(2)}) async-start(bf16[64,1,24]{2,1,0:T(2,128)(2,1)} %all_to_all.25), calls=%async_computation | async-start | bytes 65536 | tf_op jit(solution)/shard_map/all_to_all | solution.py:41
  49.3 84.1 %all-gather.3.cloned.1.call-done = bf16[512,4,512]{2,1,0:T(4,128)(2,1)} async-done(((bf16[1,4,512]{2,1,0:T(4,128)(2,1)}), bf16[512,4,512]{2,1,0:T(4,128)(2,1)}) %all-gather.3.cloned.1.call-update) | async-done | bytes 2097168 | tf_op jit(solution)/shard_map/all_gather | solution.py:13
  133.4 2.5 reshape.221
  136.0 0.0 copy-start.2
  136.0 1.9 convolution_convert_fusion.1
  137.9 11.0 %scatter_custom_fusion.2 = bf16[1536,512]{1,0:T(8,128)(2,1)} fusion(s32[1024]{0:T(1024)S(1)} %bitcast.62, bf16[128,512]{1,0:T(8,128)(2,1)S(1)} %convolution_convert_fusion.1, s32[1024]{0:T(1024)S(1)} %broadcast_clamp_fusion.1, bf16[]{:T(256)} %constant.28.clone.1), kind=kCustom, calls=%fused_computation.24 | custom fusion | bytes 1572866 | tf_op jit(solution)/shard_map/scatter | solution.py:24
  148.9 0.0 copy-done.2
  148.9 0.0 all-to-all-done
  148.9 7.9 %all-to-all-start.2 = ((bf16[64,24,512]{2,1,0:T(8,128)(2,1)}), bf16[64,24,512]{2,1,0:T(8,128)(2,1)S(1)}, u32[]{:S(2)}, u32[]{:S(2)}) async-start(bf16[64,24,512]{2,1,0:T(8,128)(2,1)} %bitcast.55), calls=%async_computation.2 | async-start | bytes 3145728 | tf_op jit(solution)/shard_map/all_to_all | solution.py:39
  156.8 14.0 %scatter_custom_fusion.1 = bf16[1536,512]{1,0:T(8,128)(2,1)} fusion(s32[1024]{0:T(1024)S(1)} %bitcast.63, bf16[128,512]{1,0:T(8,128)(2,1)} %param.8, s32[1024]{0:T(1024)S(1)} %broadcast_clamp_fusion.1, bf16[]{:T(256)} %constant.28.clone.1), kind=kCustom, calls=%fused_computation.26 | custom fusion | bytes 1573376 | tf_op jit(solution)/shard_map/scatter | solution.py:29
  170.8 25.0 %all-to-all-done.2 = bf16[64,24,512]{2,1,0:T(8,128)(2,1)S(1)} async-done(((bf16[64,24,512]{2,1,0:T(8,128)(2,1)}), bf16[64,24,512]{2,1,0:T(8,128)(2,1)S(1)}, u32[]{:S(2)}, u32[]{:S(2)}) %all-to-all-start.2) | async-done | bytes 1572896 | tf_op jit(solution)/shard_map/all_to_all | solution.py:39
  195.8 0.0 copy-start.5
  195.8 1.1 copy-done.5
  197.0 6.5 %all-to-all-start.1 = ((bf16[64,24,512]{2,1,0:T(8,128)(2,1)}), bf16[64,24,512]{2,1,0:T(8,128)(2,1)S(1)}, u32[]{:S(2)}, u32[]{:S(2)}) async-start(bf16[64,24,512]{2,1,0:T(8,128)(2,1)} %bitcast.54), calls=%async_computation.1 | async-start | bytes 3145728 | tf_op jit(solution)/shard_map/all_to_all | solution.py:40
  203.4 0.1 convert_reduce_fusion
  203.5 0.1 reshape.163
  203.6 0.0 copy-done
  203.6 5.9 fusion.7
  209.5 32.9 %all-to-all-done.1 = bf16[64,24,512]{2,1,0:T(8,128)(2,1)S(1)} async-done(((bf16[64,24,512]{2,1,0:T(8,128)(2,1)}), bf16[64,24,512]{2,1,0:T(8,128)(2,1)S(1)}, u32[]{:S(2)}, u32[]{:S(2)}) %all-to-all-start.1) | async-done | bytes 1572896 | tf_op jit(solution)/shard_map/all_to_all | solution.py:40
  242.4 0.0 copy-start.1
  242.4 5.1 fusion
  247.5 0.0 copy-done.1
  247.5 3.2 fusion.5
  250.7 6.5 %all-to-all-start.3 = ((bf16[64,24,512]{2,1,0:T(8,128)(2,1)}), bf16[64,24,512]{2,1,0:T(8,128)(2,1)S(1)}, u32[]{:S(2)}, u32[]{:S(2)}) async-start(bf16[64,24,512]{2,1,0:T(8,128)(2,1)} %bitcast.56), calls=%async_computation.3 | async-start | bytes 3145728 | tf_op jit(solution)/shard_map/all_to_all | solution.py:56
  257.2 0.0 all-reduce.3.cloned.1.call-start
  257.3 38.9 %all-to-all-done.3 = bf16[64,24,512]{2,1,0:T(8,128)(2,1)S(1)} async-done(((bf16[64,24,512]{2,1,0:T(8,128)(2,1)}), bf16[64,24,512]{2,1,0:T(8,128)(2,1)S(1)}, u32[]{:S(2)}, u32[]{:S(2)}) %all-to-all-start.3) | async-done | bytes 1572896 | tf_op jit(solution)/shard_map/all_to_all | solution.py:56
  296.2 5.1 gather_fusion
  301.3 1.9 bitcast_reduce_fusion
  303.2 0.0 copy-done.4
  303.2 2.8 convolution_bitcast_fusion
  306.0 0.0 all-reduce.3.cloned.1.call-update
  306.0 0.0 copy-start.3
  306.0 0.7 convert_element_type.57
  306.7 6.5 %all-to-all-start.4 = ((bf16[64,1,24]{2,1,0:T(2,128)(2,1)}), bf16[64,1,24]{2,1,0:T(2,128)(2,1)S(1)}, u32[]{:S(2)}, u32[]{:S(2)}) async-start(bf16[64,1,24]{2,1,0:T(2,128)(2,1)} %convert_element_type.57), calls=%async_computation.4 | async-start | bytes 65536 | tf_op jit(solution)/shard_map/all_to_all | solution.py:63
  313.2 9.3 %all-to-all-done.4 = bf16[64,1,24]{2,1,0:T(2,128)(2,1)S(1)} async-done(((bf16[64,1,24]{2,1,0:T(2,128)(2,1)}), bf16[64,1,24]{2,1,0:T(2,128)(2,1)S(1)}, u32[]{:S(2)}, u32[]{:S(2)}) %all-to-all-start.4) | async-done | bytes 3104 | tf_op jit(solution)/shard_map/all_to_all | solution.py:63
  322.6 0.1 reduce.2
  322.6 0.1 reshape.161
  322.8 6.8 %gather_fusion.1 = bf16[1024]{0:T(1024)(128)(2,1)S(1)} fusion(bf16[1536]{0:T(1024)(128)(2,1)S(1)} %reshape.161, s32[1024]{0:T(1024)S(1)} %broadcast_clamp_fusion), kind=kCustom, calls=%fused_computation.3 | custom fusion | bytes 8192 | tf_op jit(solution)/shard_map/gather | solution.py:69
  329.6 0.1 reshape.162
  329.7 0.7 copy.28
  330.3 0.0 copy-done.3
  330.3 1.6 convolution_convert_fusion
  331.9 254.3 %all-reduce.3.cloned.1.call-done = f32[2048,512]{0,1:T(8,128)} async-done(((f32[2048,512]{0,1:T(8,128)}), f32[2048,512]{0,1:T(8,128)}) %all-reduce.3.cloned.1.call-update) | async-done | bytes 4194320
  586.2 1.1 constant_dynamic-slice_fusion
  587.3 0.7 copy.27
  (8 shorter events, 0.1 us)
Async XLA Ops:
  7.2 196.5 %copy-start = (bf16[1,512,1024]{2,1,0:T(8,128)(2,1)S(1)}, bf16[1,512,1024]{2,1,0:T(8,128)(2,1)}, u32[]{:S(2)}) copy-start(bf16[1,512,1024]{2,1,0:T(8,128)(2,1)} %param.12) | copy-start | bytes 3145732
  7.2 126.3 %all-gather.3.cloned.1.call-start = ((), (), s32[]{:S(2)}) async-start(), calls=%async_computation.5 | async-start | bytes 2101248 | tf_op jit(solution)/shard_map/all_gather | solution.py:13
  37.7 111.2 %all-to-all-start = ((bf16[64,1,24]{2,1,0:T(2,128)(2,1)}), bf16[64,1,24]{2,1,0:T(2,128)(2,1)S(1)}, u32[]{:S(2)}, u32[]{:S(2)}) async-start(bf16[64,1,24]{2,1,0:T(2,128)(2,1)} %all_to_all.25), calls=%async_computation | async-start | bytes 65536 | tf_op jit(solution)/shard_map/all_to_all | solution.py:41
  136.0 12.9 %copy-start.2 = (bf16[2048,512]{1,0:T(8,128)(2,1)}, bf16[2048,512]{1,0:T(8,128)(2,1)S(1)}, u32[]{:S(2)}) copy-start(bf16[2048,512]{1,0:T(8,128)(2,1)S(1)} %reshape.221) | copy-start | bytes 6291460
  148.9 46.9 %all-to-all-start.2 = ((bf16[64,24,512]{2,1,0:T(8,128)(2,1)}), bf16[64,24,512]{2,1,0:T(8,128)(2,1)S(1)}, u32[]{:S(2)}, u32[]{:S(2)}) async-start(bf16[64,24,512]{2,1,0:T(8,128)(2,1)} %bitcast.55), calls=%async_computation.2 | async-start | bytes 3145728 | tf_op jit(solution)/shard_map/all_to_all | solution.py:39
  195.8 1.1 copy-start.5
  197.0 45.5 %all-to-all-start.1 = ((bf16[64,24,512]{2,1,0:T(8,128)(2,1)}), bf16[64,24,512]{2,1,0:T(8,128)(2,1)S(1)}, u32[]{:S(2)}, u32[]{:S(2)}) async-start(bf16[64,24,512]{2,1,0:T(8,128)(2,1)} %bitcast.54), calls=%async_computation.1 | async-start | bytes 3145728 | tf_op jit(solution)/shard_map/all_to_all | solution.py:40
  242.4 5.1 copy-start.1
  250.7 45.5 %all-to-all-start.3 = ((bf16[64,24,512]{2,1,0:T(8,128)(2,1)}), bf16[64,24,512]{2,1,0:T(8,128)(2,1)S(1)}, u32[]{:S(2)}, u32[]{:S(2)}) async-start(bf16[64,24,512]{2,1,0:T(8,128)(2,1)} %bitcast.56), calls=%async_computation.3 | async-start | bytes 3145728 | tf_op jit(solution)/shard_map/all_to_all | solution.py:56
  257.2 329.0 %all-reduce.3.cloned.1.call-start = ((), (), s32[]{:S(2)}) async-start(), calls=%async_computation.6 | async-start | bytes 8388608
  296.2 7.0 %copy-start.4 = (bf16[128,2048]{1,0:T(8,128)(2,1)S(1)}, bf16[128,2048]{1,0:T(8,128)(2,1)}, u32[]{:S(2)}) copy-start(bf16[128,2048]{1,0:T(8,128)(2,1)} %param.7) | copy-start | bytes 1572868
  306.0 24.3 %copy-start.3 = (bf16[2048,512]{1,0:T(8,128)(2,1)S(1)}, bf16[2048,512]{1,0:T(8,128)(2,1)}, u32[]{:S(2)}) copy-start(bf16[2048,512]{1,0:T(8,128)(2,1)} %copy-done.2) | copy-start | bytes 6291460
  306.7 15.8 %all-to-all-start.4 = ((bf16[64,1,24]{2,1,0:T(2,128)(2,1)}), bf16[64,1,24]{2,1,0:T(2,128)(2,1)S(1)}, u32[]{:S(2)}, u32[]{:S(2)}) async-start(bf16[64,1,24]{2,1,0:T(2,128)(2,1)} %convert_element_type.57), calls=%async_computation.4 | async-start | bytes 65536 | tf_op jit(solution)/shard_map/all_to_all | solution.py:63
Sparse Core Ops, SparseCore 0:
  12.2 121.2 all-gather.2
  306.1 280.0 all-reduce.2
where the time goes:
time: 597 us; the launch traced here: 595 us
  waiting for transfers between devices  445 us (75%)
  local copies, waits for them, and re-layouts  54.7 us (9%)
  starting transfers between devices  39 us (7%)
  other arithmetic  21.1 us (4%)
  matrix products  20.4 us (3%)
  between operations  14.3 us (2%)
    unnamed x3, waiting for transfers between devices  255 us
    all_gather x1, waiting for transfers between devices, on_device(): whole_proj = lax.all_gather(down_proj, ('dp', 'expert'), axis=0, tiled=True)  84.1 us
    all_to_all x1, waiting for transfers between devices, on_device(): lax.all_to_all(row_grad.reshape(sources, count, lat_width), 'expert', spl...  38.9 us
    all_to_all x1, waiting for transfers between devices, on_device(): lax.all_to_all(sent_grad, 'expert', split_axis=0, concat_axis=0, tiled=True)  32.9 us
    all_to_all x1, waiting for transfers between devices, on_device(): lax.all_to_all(sent_latent, 'expert', split_axis=0, concat_axis=0, tiled=...  25 us
    another operation x3, other arithmetic  18.2 us
    scatter x1, local copies, waits for them, and re-layouts, on_device(): sent_grad = jnp.zeros((experts * capacity, lat_width), jnp.bfloat16).at[s...  14 us
  transfers between devices with their start and end apart: 7, of which 6 were waited for; matrix products, arithmetic and copies ran while one was open for 13% of the time, Pallas kernels for 0%

commit v1 on v0

v1 whole, which is shorter than its diff:
```python
import functools

import jax
import jax.numpy as jnp
from jax import lax
from jax.experimental import pallas as pl
from jax.experimental.pallas import tpu as pltpu
from jax.sharding import PartitionSpec as P

MESH = pl.DeviceIdType.MESH
BF = jnp.bfloat16
F32 = jnp.float32
NC = 2


def xor(a, b, n):
    total, bit = 0, 1
    while bit < n:
        total = total + ((a // bit) % 2 + (b // bit) % 2) % 2 * bit
        bit *= 2
    return total


def nt_dot(a, b):
    return lax.dot_general(a, b, (((1,), (1,)), ((), ())), preferred_element_type=F32)


def dot(a, b):
    return jnp.dot(a, b, preferred_element_type=F32)


def remote(src, dst, sems, at, device):
    return pltpu.make_async_remote_copy(
        src_ref=src,
        dst_ref=dst,
        send_sem=sems.at[(0, *at)],
        recv_sem=sems.at[(1, *at)],
        device_id=device,
        device_id_type=MESH,
    )


def kernel(
    sizes,
    tokens, grad, routes_t, weights_t, own_rows, up, down,
    input_grad, proj_grad, weight_grad,
    proj, padded, meta, g_all, l_all, pick, back, g_send, l_send, g_got, l_got, bg,
    r_send, r_got, v_send, v_got, p_send, p_got, q_send, q_got,
    tok_far, tok_t, lsum, lsum_far, pg32, pg16, x_got, s32, s16, y_got, t16, z_got, f_send, f_got,
    sem_a, sem_b, sem_c, sem_d, sem_m, sem_g, sem_l, sem_gx, sem_lx, sem_r, sem_v, sem_p, sem_q,
    sem_tok, sem_ls, sem_x, sem_y, sem_z, sem_f,
):
    nz, ny, nx, cap = sizes
    g8 = nx * NC
    halves = nx // 2
    pairs = ny // 2
    toks = tokens.shape[0]
    lat = grad.shape[1]
    hid = up.shape[1]
    z = lax.axis_index("dp")
    e = lax.axis_index("expert")
    y = e // g8
    me8 = e % g8
    x, c = me8 // NC, me8 % NC

    def dev_z(o):
        return (xor(z, o, nz), e)

    def dev_y(o):
        return (z, xor(y, o, ny) * g8 + me8)

    def dev_8(o):
        return (z, y * g8 + xor(me8, o, g8))

    def share_of(m8):
        mx, mc = m8 // NC, m8 % NC
        return mx // 2, pl.multiple_of((mc * 2 + mx % 2) * 128, 128)

    barrier = pltpu.get_barrier_semaphore()
    for o in range(1, nz):
        pl.semaphore_signal(barrier, inc=1, device_id=dev_z(o), device_id_type=MESH)
    for o in range(1, ny):
        pl.semaphore_signal(barrier, inc=1, device_id=dev_y(o), device_id_type=MESH)
    for o in range(1, g8):
        pl.semaphore_signal(barrier, inc=1, device_id=dev_8(o), device_id_type=MESH)
    pl.semaphore_wait(barrier, nz + ny + g8 - 3)

    half, lane = share_of(me8)
    zy = z * ny + y
    sends = []

    def a_copy(o):
        _, far_lane = share_of(xor(me8, o, g8))
        return remote(own_rows.at[:, pl.ds(far_lane, 128)], padded.at[o], sem_a, (o,), dev_8(o))

    for o in range(1, 4):
        cp = a_copy(o)
        cp.start()
        sends.append(cp)

    row = lax.broadcasted_iota(jnp.int32, (ny * g8, toks), 0)
    expert = ((row // g8) ^ y) * g8 + ((row % g8) ^ me8)
    named = jnp.zeros((ny * g8, toks), F32)
    weight = jnp.zeros((ny * g8, toks), F32)
    for k in range(routes_t.shape[0]):
        hit = routes_t[k : k + 1, :] == expert
        named = jnp.where(hit, 1.0, named)
        weight = jnp.where(hit, weights_t[k : k + 1, :], weight)
    earlier = (
        lax.broadcasted_iota(jnp.int32, (toks, toks), 0)
        < lax.broadcasted_iota(jnp.int32, (toks, toks), 1)
    )
    rank = dot(named.astype(BF), jnp.where(earlier, 1.0, 0.0).astype(BF))
    rank = jnp.where(named > 0.5, rank, -1.0)
    meta[0] = jnp.concatenate(
        [rank.reshape(ny, g8, toks), weight.reshape(ny, g8, toks)], axis=1
    )

    own = own_rows[:, pl.ds(lane, 128)].astype(F32)
    for o in range(1, 4):
        a_copy(o).wait_recv()
        own = own + padded[o].astype(F32)
    proj[zy, half, :, pl.ds(lane, 128)] = own.astype(BF)

    def b_copy(o, at):
        ref = proj.at[at, half, :, pl.ds(lane, 128)]
        return remote(ref, ref, sem_b, (o,), dev_y(o))

    for o in range(1, ny):
        cp = b_copy(o, zy)
        cp.start()
        sends.append(cp)

    g_all[0] = grad[...]

    def m_copy(o):
        return remote(meta.at[0, o], meta.at[1, o], sem_m, (o,), dev_y(o))

    def g_copy(o):
        return remote(grad, g_all.at[o], sem_g, (o,), dev_y(o))

    meta[1, 0] = meta[0, 0]
    for o in range(1, ny):
        for cp in (m_copy(o), g_copy(o)):
            cp.start()
            sends.append(cp)
    tok_copy = remote(tokens, tok_far, sem_tok, (0,), dev_8(1))
    tok_copy.start()
    sends.append(tok_copy)

    for o in range(1, ny):
        b_copy(o, z * ny + xor(y, o, ny)).wait_recv()

    def c_copy(o, at_z):
        ref = proj.at[pl.ds(at_z * ny, ny), half, :, pl.ds(lane, 128)]
        return remote(ref, ref, sem_c, (o,), dev_z(o))

    for o in range(1, nz):
        cp = c_copy(o, z)
        cp.start()
        sends.append(cp)

    tok_copy.wait_recv()
    step = min(256, tokens.shape[1])

    @pl.loop(0, tokens.shape[1] // step)
    def _(n):
        at = pl.ds(pl.multiple_of(n * step, step), step)
        both = jnp.concatenate([tokens[:, at], tok_far[:, at]], axis=0)
        tok_t[at, :] = both.astype(F32).T.astype(BF)

    for o in range(1, nz):
        c_copy(o, xor(z, o, nz)).wait_recv()

    def d_copy(o, share, to):
        h, l = share_of(share)
        ref = proj.at[:, h, :, pl.ds(l, 128)]
        return remote(ref, ref, sem_d, (o,), dev_8(to))

    for o in range(2, g8, 2):
        cp = d_copy(o, me8, o)
        cp.start()
        sends.append(cp)
    cp = d_copy(1, me8, 1)
    cp.start()
    sends.append(cp)

    place = lax.broadcasted_iota(jnp.int32, (cap, toks), 0).astype(F32)

    def wait_y(copy, i):
        @pl.when(i > 0)
        def _():
            copy(2 * i).wait_recv()

        copy(2 * i + 1).wait_recv()

    def gx_copy(i, o):
        return remote(g_send.at[i, o], g_got.at[i, o], sem_gx, (i, o), dev_8(o))

    def lx_copy(i, o):
        return remote(l_send.at[i, o], l_got.at[i, o], sem_lx, (i, o), dev_8(o))

    def exchange(i, source, send, got, copy):
        both = source[pl.ds(2 * i, 2)].reshape(2 * toks, lat)
        rows = dot(pick[i], both).astype(BF).reshape(g8, 2 * cap, lat)
        got[i, 0] = rows[0]
        send[i] = rows
        for o in range(1, g8):
            copy(i, o).start()

    def pick_grad(i):
        wait_y(m_copy, i)
        wait_y(g_copy, i)
        zero = jnp.zeros((cap, toks), F32)
        weighted = []
        for o in range(g8):
            parts = []
            for s in range(2):
                ranks = meta[1, 2 * i + s, o : o + 1, :]
                parts.append(jnp.where(ranks == place, 1.0, 0.0))
            block = jnp.concatenate(
                [
                    jnp.concatenate([parts[0], zero], axis=1),
                    jnp.concatenate([zero, parts[1]], axis=1),
                ],
                axis=0,
            )
            pick[i, 2 * cap * o : 2 * cap * (o + 1), :] = block.astype(BF)
            w = jnp.concatenate(
                [meta[1, 2 * i + s, g8 + o : g8 + o + 1, :] for s in range(2)], axis=1
            )
            weighted.append(block * w)
        back[i] = jnp.concatenate(weighted, axis=0).T.astype(BF)
        exchange(i, g_all, g_send, g_got, gx_copy)

    early = pairs // 2
    pl.loop(0, early)(pick_grad)

    for o in range(2, g8, 2):
        share = xor(me8, o, g8)
        d_copy(o, share, o).wait_recv()
        cp = d_copy(o + 1, share, 1)
        cp.start()
        sends.append(cp)
    d_copy(1, xor(me8, 1, g8), 1).wait_recv()
    for o in range(2, g8, 2):
        d_copy(o + 1, xor(me8, o + 1, g8), 1).wait_recv()

    depth = tokens.shape[1]
    tile = min(256, depth)
    blocks = tile // (16 * halves)

    def proj_rows(n):
        return proj[pl.ds(n * blocks, blocks)].reshape(tile, lat)

    def latent_step(n, total):
        return total + dot(tokens[:, pl.ds(pl.multiple_of(n * tile, tile), tile)], proj_rows(n))

    latent = lax.fori_loop(0, depth // tile, latent_step, jnp.zeros((toks, lat), F32))
    l_all[0] = latent.astype(BF)

    def l_copy(o):
        return remote(l_all.at[0], l_all.at[o], sem_l, (o,), dev_y(o))

    for o in range(1, ny):
        cp = l_copy(o)
        cp.start()
        sends.append(cp)

    pl.loop(early, pairs)(pick_grad)

    wide = min(256, hid)
    many = g8 * 2 * cap
    lane_is_row = lax.broadcasted_iota(jnp.int32, (2 * cap, 128), 0) == lax.broadcasted_iota(
        jnp.int32, (2 * cap, 128), 1
    )

    def back_grad(i):
        for o in range(1, g8):
            gx_copy(i, o).wait_recv()

        @pl.loop(0, hid // wide)
        def _(n):
            at = pl.ds(pl.multiple_of(n * wide, wide), wide)
            bg[i, :, at] = nt_dot(g_got[i].reshape(many, lat), down[at, :])

    def dispatch(i):
        wait_y(l_copy, i)
        exchange(i, l_all, l_send, l_got, lx_copy)

    def r_copy(i, o):
        return remote(r_send.at[i, o], r_got.at[i, o], sem_r, (i, o), dev_8(o))

    def v_copy(i, o):
        return remote(v_send.at[i, o], v_got.at[i, o], sem_v, (i, o), dev_8(o))

    def experts(i):
        for o in range(1, g8):
            lx_copy(i, o).wait_recv()
        rows = l_got[i].reshape(many, lat)

        def unit_step(n, carry):
            total, sums = carry
            at = pl.ds(pl.multiple_of(n * wide, wide), wide)
            active = jnp.maximum(dot(rows, up[:, at]), 0.0)
            part = bg[i, :, at] * active
            sums = sums + jnp.sum(part * active, axis=1, keepdims=True)
            return total + nt_dot((2.0 * part).astype(BF), up[:, at]), sums

        total, sums = lax.fori_loop(
            0, hid // wide, unit_step, (jnp.zeros((many, lat), F32), jnp.zeros((many, 1), F32))
        )
        out = total.astype(BF).reshape(g8, 2 * cap, lat)
        r_got[i, 0] = out[0]
        r_send[i] = out
        for o in range(g8):
            column = sums[2 * cap * o : 2 * cap * (o + 1)]
            line = jnp.sum(jnp.where(lane_is_row, column, 0.0), axis=0, keepdims=True)
            line = jnp.broadcast_to(line, (8, 128))
            if o == 0:
                v_got[i, 0] = line
            else:
                v_send[i, o] = line
        for o in range(1, g8):
            r_copy(i, o).start()
            v_copy(i, o).start()

    def p_copy(o):
        return remote(p_send.at[o], p_got.at[o], sem_p, (o,), dev_y(o))

    def q_copy(o):
        return remote(q_send.at[o], q_got.at[o], sem_q, (o,), dev_y(o))

    def combine(i):
        for o in range(1, g8):
            r_copy(i, o).wait_recv()
            v_copy(i, o).wait_recv()
        part = dot(back[i], r_got[i].reshape(many, lat)).astype(BF)
        lines = []
        for o in range(g8):
            column = jnp.sum(
                jnp.where(lane_is_row, v_got[i, o, 0:1, :], 0.0), axis=1, keepdims=True
            )
            block = pick[i, 2 * cap * o : 2 * cap * (o + 1), :].astype(F32)
            lines.append(jnp.sum(block * column, axis=0, keepdims=True))
        sums = jnp.concatenate(lines, axis=0)
        p_send[pl.ds(2 * i, 2)] = part.reshape(2, toks, lat)
        for s in range(2):
            q_send[2 * i + s] = sums[:, s * toks : (s + 1) * toks]

        @pl.when(i > 0)
        def _():
            p_copy(2 * i).start()
            q_copy(2 * i).start()

        p_copy(2 * i + 1).start()
        q_copy(2 * i + 1).start()

    @pl.loop(0, pairs + 2)
    def _(k):
        @pl.when(k < pairs)
        def _():
            back_grad(k)
            dispatch(k)

        @pl.when((k >= 1) & (k < pairs + 1))
        def _():
            experts(k - 1)

        @pl.when(k >= 2)
        def _():
            combine(k - 2)

    total = p_send[0].astype(F32)
    for o in range(1, ny):
        p_copy(o).wait_recv()
        total = total + p_got[o].astype(F32)
    lsum[...] = total.astype(BF)
    side = lat // 2
    far_side = pl.ds(pl.multiple_of((1 - c) * side, side), side)
    my_side = pl.ds(pl.multiple_of(c * side, side), side)
    ls_copy = remote(lsum.at[:, far_side], lsum_far, sem_ls, (0,), dev_8(1))
    ls_copy.start()
    sends.append(ls_copy)

    for o in range(1, ny):
        q_copy(o).wait_recv()
    q_got[0] = q_send[0]
    sums = q_got[...].reshape(ny * g8, toks)
    for k in range(routes_t.shape[0]):
        hit = routes_t[k : k + 1, :] == expert
        weight_grad[k : k + 1, :] = jnp.sum(jnp.where(hit, sums, 0.0), axis=0, keepdims=True)

    ls_copy.wait_recv()
    mine, far = lsum[:, my_side], lsum_far[...]
    pair_sum = jnp.concatenate([mine, far], axis=0)

    @pl.loop(0, depth // tile)
    def _(n):
        at = pl.ds(pl.multiple_of(n * tile, tile), tile)
        part = dot(tok_t[at, :], pair_sum).reshape(blocks, halves, 16, side)
        pg32[pl.ds(n * blocks, blocks)] = part
        pg16[pl.ds(n * blocks, blocks)] = part.astype(BF)

    def x_lane(m8):
        return pl.ds(pl.multiple_of((m8 // NC) % 2 * 128, 128), 128)

    def x_copy(o):
        far8 = xor(me8, 2 * o, g8)
        src = pg16.at[:, far8 // NC // 2, :, x_lane(far8)]
        return remote(src, x_got.at[o], sem_x, (o,), dev_8(2 * o))

    for o in range(1, nx):
        cp = x_copy(o)
        cp.start()
        sends.append(cp)

    @pl.loop(0, depth // tile)
    def _(n):
        at = pl.ds(pl.multiple_of(n * tile, tile), tile)
        input_grad[:, at] = nt_dot(lsum[...], proj_rows(n)).astype(BF)

    total = pg32[:, half, :, x_lane(me8)]
    for o in range(1, nx):
        x_copy(o).wait_recv()
        total = total + x_got[o].astype(F32)
    total = total.reshape(nz, ny, 16, 128)
    s32[...] = total
    s16[...] = total.astype(BF)

    def y_copy(o):
        return remote(s16.at[:, xor(y, o, ny)], y_got.at[o], sem_y, (o,), dev_y(o))

    for o in range(1, ny):
        cp = y_copy(o)
        cp.start()
        sends.append(cp)
    total = s32[:, y]
    for o in range(1, ny):
        y_copy(o).wait_recv()
        total = total + y_got[o].astype(F32)
    t16[...] = total.astype(BF)
    s32[:, 0] = total

    def z_copy(o):
        return remote(t16.at[xor(z, o, nz)], z_got.at[o], sem_z, (o,), dev_z(o))

    for o in range(1, nz):
        cp = z_copy(o)
        cp.start()
        sends.append(cp)
    total = s32[z, 0]
    for o in range(1, nz):
        z_copy(o).wait_recv()
        total = total + z_got[o].astype(F32)
    f_send[...] = total
    f_got[:, pl.ds(lane, 128)] = total

    def f_copy(o, m8):
        _, l = share_of(m8)
        return remote(f_send, f_got.at[:, pl.ds(l, 128)], sem_f, (o,), dev_8(o))

    for o in range(1, 4):
        cp = f_copy(o, me8)
        cp.start()
        sends.append(cp)
    for o in range(1, 4):
        f_copy(o, xor(me8, o, g8)).wait_recv()
    rows = jnp.zeros((4, lat), F32)
    for k in range(4):
        rows = rows + jnp.where(me8 % 4 == k, f_got[4 * k : 4 * k + 4, :], 0.0)
    proj_grad[...] = rows

    for cp in sends:
        cp.wait_send()

    @pl.loop(0, pairs)
    def _(i):
        for o in range(1, g8):
            for copy in (gx_copy, lx_copy, r_copy, v_copy):
                copy(i, o).wait_send()

    for o in range(1, ny):
        p_copy(o).wait_send()
        q_copy(o).wait_send()


def on_device(sizes, tokens, latent_grad, routes, route_weights, down_proj, expert_up, expert_down):
    nz, ny, nx, cap = sizes
    toks, depth = tokens.shape
    top = routes.shape[1]
    lat = latent_grad.shape[1]
    hid = expert_up.shape[2]
    g8, halves, pairs = nx * NC, nx // 2, ny // 2
    many = 2 * cap * g8
    e = lax.axis_index("expert")
    place = jnp.arange(16, dtype=jnp.int32) // 4
    own_rows = jnp.where((place == e % 4)[:, None], jnp.tile(down_proj, (4, 1)), 0).astype(BF)
    vmem = pl.BlockSpec(memory_space=pltpu.VMEM)
    dma = pltpu.SemaphoreType.DMA
    buffers = [
        pltpu.VMEM((nz * ny, halves, 16, lat), BF),
        pltpu.VMEM((4, 16, 128), BF),
        pltpu.VMEM((2, ny, 2 * g8, toks), F32),
        pltpu.VMEM((ny, toks, lat), BF),
        pltpu.VMEM((ny, toks, lat), BF),
        pltpu.VMEM((pairs, many, 2 * toks), BF),
        pltpu.VMEM((pairs, 2 * toks, many), BF),
        pltpu.VMEM((pairs, g8, 2 * cap, lat), BF),
        pltpu.VMEM((pairs, g8, 2 * cap, lat), BF),
        pltpu.VMEM((pairs, g8, 2 * cap, lat), BF),
        pltpu.VMEM((pairs, g8, 2 * cap, lat), BF),
        pltpu.VMEM((pairs, many, hid), F32),
        pltpu.VMEM((pairs, g8, 2 * cap, lat), BF),
        pltpu.VMEM((pairs, g8, 2 * cap, lat), BF),
        pltpu.VMEM((pairs, g8, 8, 128), F32),
        pltpu.VMEM((pairs, g8, 8, 128), F32),
        pltpu.VMEM((ny, toks, lat), BF),
        pltpu.VMEM((ny, toks, lat), BF),
        pltpu.VMEM((ny, g8, toks), F32),
        pltpu.VMEM((ny, g8, toks), F32),
        pltpu.VMEM((toks, depth), BF),
        pltpu.VMEM((depth, 2 * toks), BF),
        pltpu.VMEM((toks, lat), BF),
        pltpu.VMEM((toks, lat // 2), BF),
        pltpu.VMEM((nz * ny, halves, 16, lat // 2), F32),
        pltpu.VMEM((nz * ny, halves, 16, lat // 2), BF),
        pltpu.VMEM((nx, nz * ny, 16, 128), BF),
        pltpu.VMEM((nz, ny, 16, 128), F32),
        pltpu.VMEM((nz, ny, 16, 128), BF),
        pltpu.VMEM((ny, nz, 16, 128), BF),
        pltpu.VMEM((nz, 16, 128), BF),
        pltpu.VMEM((nz, 16, 128), BF),
        pltpu.VMEM((16, 128), F32),
        pltpu.VMEM((16, lat), F32),
    ]
    counts = [
        (4,), (ny,), (nz,), (g8,), (ny,), (ny,), (ny,),
        (pairs, g8), (pairs, g8), (pairs, g8), (pairs, g8), (ny,), (ny,),
        (1,), (1,), (nx,), (ny,), (nz,), (4,),
    ]
    input_grad, proj_grad, weight_grad = pl.pallas_call(
        functools.partial(kernel, sizes),
        out_shape=[
            jax.ShapeDtypeStruct((toks, depth), BF),
            jax.ShapeDtypeStruct((4, lat), F32),
            jax.ShapeDtypeStruct((top, toks), F32),
        ],
        in_specs=[vmem] * 7,
        out_specs=[vmem] * 3,
        scratch_shapes=buffers + [dma((2, *count)) for count in counts],
        compiler_params=pltpu.CompilerParams(
            collective_id=0, has_side_effects=True, vmem_limit_bytes=56 * 1024 * 1024
        ),
    )(
        tokens,
        latent_grad,
        routes.T,
        route_weights.astype(F32).T,
        own_rows,
        expert_up[0],
        expert_down[0],
    )
    return input_grad, proj_grad, weight_grad.T.astype(BF)


def build(mesh, nx, cap):
    nz, experts = mesh.shape["dp"], mesh.shape["expert"]
    sizes = (nz, experts // (nx * NC), nx, cap)
    both = P(("dp", "expert"), None)
    one = P("expert", None, None)
    return jax.shard_map(
        functools.partial(on_device, sizes),
        mesh=mesh,
        in_specs=(both, both, both, both, both, one, one),
        out_specs=(both, both, both),
        check_vma=False,
    )


def solution(mesh):
    return build(mesh, 4, 24)
```

time: 597 us -> 172 us (0.29)
  waiting for transfers between devices: 445 us -> 0 us
  Pallas kernels: 0 us -> 165 us
  local copies, waits for them, and re-layouts: 54.7 us -> 3.85 us
  starting transfers between devices: 39 us -> 0 us
  matrix products: 20.4 us -> 0 us
  other arithmetic: 21.1 us -> 1.86 us
  between operations: 14.3 us -> 0.69 us
    unnamed x3 -> x0, waiting for transfers between devices: 255 us -> none
    pallas_call x0 -> x1, Pallas kernels: none -> 165 us  [on_device(): pl.pallas_call(functools.partial(kernel, sizes), out_shape=[jax.ShapeDtyp...]
    all_to_all x5 -> x0, waiting for transfers between devices: 106 us -> none  [the longest x1 38.9 us: on_device(): lax.all_to_all(row_grad.reshape(sources, count, lat_width), 'expert', spl...]
    all_gather x1 -> x0, waiting for transfers between devices: 84.1 us -> none  [on_device(): whole_proj = lax.all_gather(down_proj, ('dp', 'expert'), axis=0, tiled=True)]
    all_to_all x5 -> x0, starting transfers between devices: 38.9 us -> none  [the longest x1 11.6 us: on_device(): lax.all_to_all(sent_weight, 'expert', split_axis=0, concat_axis=0, tiled=...]
    scatter x3 -> x0, local copies, waits for them, and re-layouts: 32.6 us -> none  [the longest x1 14 us: on_device(): sent_grad = jnp.zeros((experts * capacity, lat_width), jnp.bfloat16).at[s...]
    dot_general x6 -> x0, matrix products: 20.4 us -> none  [the longest x1 5.9 us: on_device(): jnp.dot(rows_latent, up_matrix, preferred_element_type=jnp.float32)]
    another operation x3 -> x0, other arithmetic: 18.2 us -> none
  transfers between devices with their start and end apart: 7 -> 0, of which waited for: 6 -> 0; matrix products, arithmetic and copies ran while one was open for 13% -> 0% of each run, Pallas kernels for 0% -> 0%
where the time goes in v1:
time: 172 us; the launch traced here: 171 us
  Pallas kernels  165 us (96%)
  local copies, waits for them, and re-layouts  3.85 us (2%)
  other arithmetic  1.86 us (1%)
    pallas_call x1, Pallas kernels, on_device(): pl.pallas_call(functools.partial(kernel, sizes), out_shape=[jax.ShapeDtyp...  165 us
    unnamed x10, local copies, waits for them, and re-layouts  3.83 us

profile of v1, /device:TPU:1, one launch (start us, length us, event | category | flops | bytes accessed | tf_op | source)
XLA Modules:
  0.0 171.5 jit_solution(1560240861396746402)
XLA Ops:
  0.7 0.0 copy-start.3
  0.7 0.0 copy-start.1
  0.7 0.7 copy-done.3
  1.3 0.6 convert_bitcast_fusion.weights_t
  1.9 0.0 copy-done.1
  2.0 0.7 broadcast_select_fusion.own_rows
  2.6 165.1 %shard_map.94 = (bf16[128,2048]{1,0:T(8,128)(2,1)}, f32[4,512]{1,0:T(4,128)}, f32[8,128]{1,0:T(8,128)}) custom-call(bf16[128,2048]{1,0:T(8,128)(2,1)} %tokens.1, bf16[128,512]{1,0:T(8,128)(2,1)} %grad.1, s32[8,128]{1,0:T(8,128)} %bitcast.9, f32[8,128]{1,0:T(8,128)} %convert_bitcast_fusion.weights_t, bf16[16,512]{1,0:T(8,128)(2,1)} %broadcast_select_fusion.own_rows, ...), custom_call_target="tpu_custom_call" | custom-call | tf_op jit(solution)/shard_map/pallas_call | solution.py:542
  167.7 0.0 copy-start.2
  167.7 0.7 copy-done.2
  168.4 0.6 convert_bitcast_fusion.1
  169.0 0.0 copy-start
  169.0 1.9 %copy.12 = bf16[128,2048]{1,0:T(8,128)(2,1)} copy(bf16[128,2048]{1,0:T(8,128)(2,1)} %get-tuple-element.12) | data formatting | bytes 1048576
  170.9 0.0 copy-done
  170.9 0.6 copy.13
  (3 shorter events, 0.0 us)
Async XLA Ops:
  0.7 0.7 copy-start.3
  0.7 1.3 copy-start.1
  167.7 0.7 copy-start.2
  169.0 1.9 %copy-start = (f32[4,512]{1,0:T(4,128)S(1)}, f32[4,512]{1,0:T(4,128)}, u32[]{:S(2)}) copy-start(f32[4,512]{1,0:T(4,128)} %get-tuple-element.13) | copy-start | bytes 24580

commit v2 on v1

v2 whole, which is shorter than its diff:
```python
import functools

import jax
import jax.numpy as jnp
from jax import lax
from jax.experimental import pallas as pl
from jax.experimental.pallas import tpu as pltpu
from jax.sharding import PartitionSpec as P

MESH = pl.DeviceIdType.MESH
BF = jnp.bfloat16
F32 = jnp.float32
NC = 2


def xor(a, b, n):
    total, bit = 0, 1
    while bit < n:
        total = total + ((a // bit) % 2 + (b // bit) % 2) % 2 * bit
        bit *= 2
    return total


def nt_dot(a, b):
    return lax.dot_general(a, b, (((1,), (1,)), ((), ())), preferred_element_type=F32)


def dot(a, b):
    return jnp.dot(a, b, preferred_element_type=F32)


def remote(src, dst, sems, at, device):
    return pltpu.make_async_remote_copy(
        src_ref=src,
        dst_ref=dst,
        send_sem=sems.at[(0, *at)],
        recv_sem=sems.at[(1, *at)],
        device_id=device,
        device_id_type=MESH,
    )


def kernel(
    sizes,
    tokens_in, grad, routes_t, weights_t, own_rows, up_in, down_in,
    input_grad, proj_grad, weight_grad,
    tokens, up, down, units, order, proj, latent,
    meta, g_all, l_all, pick, back, g_send, l_send, g_got, l_got, bg,
    r_send, r_got, v_send, v_got, p_send, p_got, q_send, q_got,
    tok_far, tok_t, lsum, lsum_far, pg32, pg16, x_got, s32, s16, y_got, z32, z_got, f_send, f_got,
    sem_in, sem_b, sem_c, sem_d, sem_e, sem_m, sem_g, sem_l, sem_gx, sem_lx, sem_r, sem_v, sem_p,
    sem_q, sem_tok, sem_ls, sem_x, sem_y, sem_z, sem_f,
):
    nz, ny, nx, cap = sizes
    g8 = nx * NC
    pairs = ny // 2
    toks, depth = tokens.shape
    lat = grad.shape[1]
    hid = up.shape[1]
    z = lax.axis_index("dp")
    e = lax.axis_index("expert")
    y = e // g8
    me8 = e % g8
    x, c = me8 // NC, me8 % NC

    def dev_z(o):
        return (xor(z, o, nz), e)

    def dev_y(o):
        return (z, xor(y, o, ny) * g8 + me8)

    def dev_step(d):
        return (z, (y + d + ny) % ny * g8 + me8)

    def dev_8(o):
        return (z, y * g8 + xor(me8, o, g8))

    loads = [
        pltpu.make_async_copy(src, dst, sem_in.at[k])
        for k, (src, dst) in enumerate(((tokens_in, tokens), (down_in, down), (up_in, up)))
    ]
    for cp in loads:
        cp.start()
    barrier = pltpu.get_barrier_semaphore()
    for o in range(1, nz):
        pl.semaphore_signal(barrier, inc=1, device_id=dev_z(o), device_id_type=MESH)
    for o in range(1, ny):
        pl.semaphore_signal(barrier, inc=1, device_id=dev_y(o), device_id_type=MESH)
    for o in range(1, g8):
        pl.semaphore_signal(barrier, inc=1, device_id=dev_8(o), device_id_type=MESH)

    own = own_rows[...].astype(F32)
    quarters = lat // 128
    units[c, x, z, y] = jnp.concatenate(
        [own[:, 128 * k : 128 * (k + 1)] for k in range(quarters)], axis=0
    ).astype(BF)

    row = lax.broadcasted_iota(jnp.int32, (ny * g8, toks), 0)
    slot = row // g8
    away = jnp.where(slot % 2 == 0, slot // 2 + 1, -(slot // 2) - 1)
    away = jnp.where(slot == ny - 2, 0, away)
    expert = ((y + away + ny) % ny) * g8 + ((row % g8) ^ me8)
    named = jnp.zeros((ny * g8, toks), F32)
    weight = jnp.zeros((ny * g8, toks), F32)
    weights = weights_t[...].astype(F32)
    for k in range(routes_t.shape[0]):
        hit = routes_t[k : k + 1, :] == expert
        named = jnp.where(hit, 1.0, named)
        weight = jnp.where(hit, weights[k : k + 1, :], weight)
    earlier = (
        lax.broadcasted_iota(jnp.int32, (toks, toks), 0)
        < lax.broadcasted_iota(jnp.int32, (toks, toks), 1)
    )
    rank = dot(named.astype(BF), jnp.where(earlier, 1.0, 0.0).astype(BF))
    rank = jnp.where(named > 0.5, rank, -1.0)
    meta[0] = jnp.concatenate(
        [rank.reshape(ny, g8, toks), weight.reshape(ny, g8, toks)], axis=1
    )
    meta[1, ny - 2] = meta[0, ny - 2]
    g_all[ny - 2] = grad[...]

    block = NC * nx * 2 * 16
    to = lax.broadcasted_iota(jnp.int32, (block, block), 0)
    rest = to % (block // 4)
    origin = (
        ((rest // 4 % NC) * nx + rest // (4 * NC) % nx) * 2 + rest // (4 * NC * nx)
    ) * 16 + to // (block // 4) * 4 + rest % 4
    hit = origin == lax.broadcasted_iota(jnp.int32, (block, block), 1)
    order[...] = jnp.where(hit, 1.0, 0.0).astype(BF)

    pl.semaphore_wait(barrier, nz + ny + g8 - 3)

    sends = []

    def start(cp):
        cp.start()
        sends.append(cp)

    def b_copy(o, at_y):
        ref = units.at[c, x, z, at_y]
        return remote(ref, ref, sem_b, (o,), dev_y(o))

    def c_copy(o, at_z):
        ref = units.at[c, x, at_z]
        return remote(ref, ref, sem_c, (o,), dev_z(o))

    def d_copy(o, ox, at_x):
        ref = units.at[c, at_x, xor(z, o, nz)]
        return remote(ref, ref, sem_d, (o, ox), dev_8(2 * ox))

    def e_copy(o, ox, at_c):
        ref = units.at[at_c, xor(x, ox, nx), xor(z, o, nz)]
        return remote(ref, ref, sem_e, (o, ox), dev_8(1))

    for o in range(1, ny):
        start(b_copy(o, y))

    def m_even(i):
        return remote(
            meta.at[0, 2 * i], meta.at[1, 2 * i + 1], sem_m, (2 * i + 1,), dev_step(i + 1)
        )

    def m_odd(i):
        to = 2 * i + i // (pairs - 1)
        return remote(meta.at[0, 2 * i + 1], meta.at[1, to], sem_m, (to,), dev_step(-i - 1))

    for i in range(pairs):
        if i < pairs - 1:
            start(m_even(i))
        start(m_odd(i))

    def y_near(rows, sem, s):
        away = (1, -1, 2, -2)[s]
        return remote(rows.at[ny - 2], rows.at[s], sem, (s,), dev_step(-away))

    def y_far(rows, sem, s):
        if s < 6:
            return remote(rows.at[s - 2], rows.at[s], sem, (s,), dev_step((-1, 1)[s - 4]))
        at = pl.ds((7 - s) * (toks // 2), toks // 2)
        return remote(
            rows.at[(2, 3)[s - 6], at], rows.at[7, at], sem, (s,), dev_step((-2, 2)[s - 6])
        )

    def y_start(rows, sem):
        for s in range(4):
            start(y_near(rows, sem, s))

    def y_wait(rows, sem, i):
        @pl.when(i < 2)
        def _():
            for k in range(2):
                @pl.when(i == k)
                def _():
                    y_near(rows, sem, 2 * k).wait_recv()
                    y_near(rows, sem, 2 * k + 1).wait_recv()

        @pl.when(i == 1)
        def _():
            for s in range(4, 8):
                y_far(rows, sem, s).start()

        for k in range(2, 4):
            @pl.when(i == k)
            def _():
                y_far(rows, sem, 2 * k).wait_recv()
                y_far(rows, sem, 2 * k + 1).wait_recv()

    y_start(g_all, sem_g)
    loads[0].wait()
    tok_copy = remote(tokens, tok_far, sem_tok, (0,), dev_8(1))
    start(tok_copy)

    for o in range(1, ny):
        b_copy(o, xor(y, o, ny)).wait_recv()
    for o in range(1, nz):
        start(c_copy(o, z))

    @pl.loop(0, nz)
    def _(o):
        @pl.when(o > 0)
        def _():
            c_copy(o, xor(z, o, nz)).wait_recv()

        for ox in range(1, nx):
            d_copy(o, ox, x).start()
        e_copy(o, 0, c).start()

    tok_copy.wait_recv()
    tile = depth // nz

    @pl.loop(0, nz)
    def _(n):
        at = pl.ds(pl.multiple_of(n * tile, tile), tile)
        both = jnp.concatenate([tokens[:, at], tok_far[:, at]], axis=0)
        tok_t[at, :] = both.astype(F32).T.astype(BF)

    place = lax.broadcasted_iota(jnp.int32, (cap, toks), 0).astype(F32)

    def gx_copy(i, o):
        return remote(g_send.at[i, o], g_got.at[i, o], sem_gx, (i, o), dev_8(o))

    def lx_copy(i, o):
        return remote(l_send.at[i, o], l_got.at[i, o], sem_lx, (i, o), dev_8(o))

    def exchange(i, source, send, got, copy):
        both = source[pl.ds(2 * i, 2)].reshape(2 * toks, lat)
        rows = dot(pick[i], both).astype(BF).reshape(g8, 2 * cap, lat)
        got[i, 0] = rows[0]
        send[i] = rows
        for o in range(1, g8):
            copy(i, o).start()

    def pick_grad(i):
        zero = jnp.zeros((cap, toks), F32)
        weighted = []
        for o in range(g8):
            parts = []
            for s in range(2):
                ranks = meta[1, 2 * i + s, o : o + 1, :]
                parts.append(jnp.where(ranks == place, 1.0, 0.0))
            block = jnp.concatenate(
                [
                    jnp.concatenate([parts[0], zero], axis=1),
                    jnp.concatenate([zero, parts[1]], axis=1),
                ],
                axis=0,
            )
            pick[i, 2 * cap * o : 2 * cap * (o + 1), :] = block.astype(BF)
            w = jnp.concatenate(
                [meta[1, 2 * i + s, g8 + o : g8 + o + 1, :] for s in range(2)], axis=1
            )
            weighted.append(block * w)
        exchange(i, g_all, g_send, g_got, gx_copy)
        back[i] = jnp.concatenate(weighted, axis=0).T.astype(BF)

    for i in range(pairs):
        if i < pairs - 1:
            m_even(i).wait_recv()
        m_odd(i).wait_recv()
    for i in range(2):
        y_wait(g_all, sem_g, i)
    pl.loop(0, 2)(pick_grad)

    latent[...] = jnp.zeros_like(latent)

    @pl.loop(0, nz + 1)
    def _(k):
        @pl.when(k < nz)
        def _():
            for ox in range(1, nx):
                d_copy(k, ox, xor(x, ox, nx)).wait_recv()
                e_copy(k, ox, c).start()

        @pl.when(k > 0)
        def _():
            o = k - 1
            for ox in range(nx):
                e_copy(o, ox, 1 - c).wait_recv()
            at_z = xor(z, o, nz)
            for h in range(ny // 2):
                mixed = units[:, :, at_z, 2 * h : 2 * h + 2].reshape(block, 128)
                ordered = dot(order[...], mixed).astype(BF)
                for q in range(quarters):
                    rows = ordered[block // 4 * q : block // 4 * (q + 1)]
                    proj[at_z, h, :, 128 * q : 128 * (q + 1)] = rows
            at = pl.ds(pl.multiple_of(at_z * tile, tile), tile)
            latent[...] += dot(tokens[:, at], proj[at_z].reshape(tile, lat))

    l_all[ny - 2] = latent[...].astype(BF)
    y_start(l_all, sem_l)

    @pl.loop(2, pairs)
    def _(i):
        y_wait(g_all, sem_g, i)
        pick_grad(i)

    loads[1].wait()
    loads[2].wait()
    wide = min(256, hid)
    many = g8 * 2 * cap
    lane_is_row = lax.broadcasted_iota(jnp.int32, (2 * cap, 128), 0) == lax.broadcasted_iota(
        jnp.int32, (2 * cap, 128), 1
    )

    def back_grad(i):
        for o in range(1, g8):
            gx_copy(i, o).wait_recv()

        @pl.loop(0, hid // wide)
        def _(n):
            at = pl.ds(pl.multiple_of(n * wide, wide), wide)
            bg[i, :, at] = nt_dot(g_got[i].reshape(many, lat), down[at, :])

    def dispatch(i):
        y_wait(l_all, sem_l, i)
        exchange(i, l_all, l_send, l_got, lx_copy)

    def r_copy(i, o):
        return remote(r_send.at[i, o], r_got.at[i, o], sem_r, (i, o), dev_8(o))

    def v_copy(i, o):
        return remote(v_send.at[i, o], v_got.at[i, o], sem_v, (i, o), dev_8(o))

    def experts(i):
        for o in range(1, g8):
            lx_copy(i, o).wait_recv()
        rows = l_got[i].reshape(many, lat)

        def unit_step(n, carry):
            total, sums = carry
            at = pl.ds(pl.multiple_of(n * wide, wide), wide)
            active = jnp.maximum(dot(rows, up[:, at]), 0.0)
            part = bg[i, :, at] * active
            sums = sums + jnp.sum(part * active, axis=1, keepdims=True)
            return total + nt_dot((2.0 * part).astype(BF), up[:, at]), sums

        total, sums = lax.fori_loop(
            0, hid // wide, unit_step, (jnp.zeros((many, lat), F32), jnp.zeros((many, 1), F32))
        )
        out = total.astype(BF).reshape(g8, 2 * cap, lat)
        r_got[i, 0] = out[0]
        r_send[i] = out
        for o in range(1, g8):
            r_copy(i, o).start()
        for o in range(g8):
            column = sums[2 * cap * o : 2 * cap * (o + 1)]
            line = jnp.sum(jnp.where(lane_is_row, column, 0.0), axis=0, keepdims=True)
            line = jnp.broadcast_to(line, (8, 128))
            if o == 0:
                v_got[i, 0] = line
            else:
                v_send[i, o] = line
        for o in range(1, g8):
            v_copy(i, o).start()

    def p_even(i):
        return remote(
            p_send.at[2 * i], p_got.at[2 * i + 1], sem_p, (2 * i + 1,), dev_step(i + 1)
        )

    def p_odd(i):
        to = 2 * i + i // (pairs - 1)
        return remote(p_send.at[2 * i + 1], p_got.at[to], sem_p, (to,), dev_step(-i - 1))

    def q_even(i):
        return remote(
            q_send.at[2 * i], q_got.at[2 * i + 1], sem_q, (2 * i + 1,), dev_step(i + 1)
        )

    def q_odd(i):
        to = 2 * i + i // (pairs - 1)
        return remote(q_send.at[2 * i + 1], q_got.at[to], sem_q, (to,), dev_step(-i - 1))

    def combine(i):
        for o in range(1, g8):
            r_copy(i, o).wait_recv()
        part = dot(back[i], r_got[i].reshape(many, lat)).astype(BF)
        p_send[pl.ds(2 * i, 2)] = part.reshape(2, toks, lat)

        @pl.when(i < pairs - 1)
        def _():
            p_even(i).start()

        p_odd(i).start()
        for o in range(1, g8):
            v_copy(i, o).wait_recv()
        lines = []
        for o in range(g8):
            column = jnp.sum(
                jnp.where(lane_is_row, v_got[i, o, 0:1, :], 0.0), axis=1, keepdims=True
            )
            block = pick[i, 2 * cap * o : 2 * cap * (o + 1), :].astype(F32)
            lines.append(jnp.sum(block * column, axis=0, keepdims=True))
        sums = jnp.concatenate(lines, axis=0)
        for s in range(2):
            q_send[2 * i + s] = sums[:, s * toks : (s + 1) * toks]

        @pl.when(i < pairs - 1)
        def _():
            q_even(i).start()

        q_odd(i).start()

    @pl.loop(0, pairs + 2)
    def _(k):
        @pl.when(k < pairs)
        def _():
            dispatch(k)
            back_grad(k)

        @pl.when((k >= 1) & (k < pairs + 1))
        def _():
            experts(k - 1)

        @pl.when(k >= 2)
        def _():
            combine(k - 2)

    total = p_send[ny - 2].astype(F32)
    for i in range(pairs):
        if i < pairs - 1:
            p_even(i).wait_recv()
            total = total + p_got[2 * i + 1].astype(F32)
        p_odd(i).wait_recv()
        total = total + p_got[2 * i + i // (pairs - 1)].astype(F32)
    lsum[...] = total.astype(BF)
    side = lat // 2
    far_side = pl.ds(pl.multiple_of((1 - c) * side, side), side)
    my_side = pl.ds(pl.multiple_of(c * side, side), side)
    ls_copy = remote(lsum.at[:, far_side], lsum_far, sem_ls, (0,), dev_8(1))
    start(ls_copy)

    @pl.loop(0, nz)
    def _(n):
        at = pl.ds(pl.multiple_of(n * tile, tile), tile)
        input_grad[:, at] = nt_dot(lsum[...], proj[n].reshape(tile, lat)).astype(BF)

    ls_copy.wait_recv()
    pair_sum = jnp.concatenate([lsum[:, my_side], lsum_far[...]], axis=0)

    def x_copy(n, ox):
        src = pg16.at[n, xor(x, ox, nx)]
        return remote(src, x_got.at[ox, n], sem_x, (n, ox), dev_8(2 * ox))

    @pl.loop(0, nz)
    def _(n):
        at = pl.ds(pl.multiple_of(n * tile, tile), tile)
        part = dot(tok_t[at, :], pair_sum).reshape(ny, nx, 8, side)
        for k in range(nx):
            piece = part[:, k].reshape(ny * 8, side)
            pg32[n, k] = piece
            pg16[n, k] = piece.astype(BF)
        for ox in range(1, nx):
            x_copy(n, ox).start()

    for i in range(pairs):
        if i < pairs - 1:
            q_even(i).wait_recv()
        q_odd(i).wait_recv()
    q_got[ny - 2] = q_send[ny - 2]
    sums = q_got[...].reshape(ny * g8, toks)
    lines = []
    for k in range(routes_t.shape[0]):
        hit = routes_t[k : k + 1, :] == expert
        lines.append(jnp.sum(jnp.where(hit, sums, 0.0), axis=0, keepdims=True))
    weight_grad[...] = jnp.concatenate(lines, axis=0).astype(BF)

    def y_copy(p, o):
        src = s16.at[p, xor(y, o, ny)]
        return remote(src, y_got.at[o, p], sem_y, (p, o), dev_y(o))

    @pl.loop(0, nz // 2)
    def _(p):
        halves = []
        for s in range(2):
            n = 2 * p + s
            total = pg32[n, x]
            for ox in range(1, nx):
                x_copy(n, ox).wait_recv()
                total = total + x_got[ox, n].astype(F32)
            halves.append(total.reshape(ny, 1, 8, side))
        both = jnp.concatenate(halves, axis=1).reshape(ny, 16, side)
        s32[p] = both
        s16[p] = both.astype(BF)
        for o in range(1, ny):
            y_copy(p, o).start()

    @pl.loop(0, nz // 2)
    def _(p):
        total = s32[p, y]
        for o in range(1, ny):
            y_copy(p, o).wait_recv()
            total = total + y_got[o, p].astype(F32)
        z32[pl.ds(2 * p, 2)] = total.reshape(2, 8, side)

    def z_copy(o):
        return remote(z32.at[xor(z, o, nz)], z_got.at[o], sem_z, (o,), dev_z(o))

    for o in range(1, nz):
        start(z_copy(o))
    total = z32[z]
    for o in range(1, nz):
        z_copy(o).wait_recv()
        total = total + z_got[o]
    f_send[...] = total
    f_copy = remote(f_send, f_got, sem_f, (0,), dev_8(1))
    start(f_copy)
    proj_grad[:, my_side] = jnp.where(c == 0, total[:4], total[4:])
    f_copy.wait_recv()
    proj_grad[:, far_side] = jnp.where(c == 0, f_got[:4, :], f_got[4:, :])

    for cp in sends:
        cp.wait_send()
    for rows, sem in ((g_all, sem_g), (l_all, sem_l)):
        for s in range(4, 8):
            y_far(rows, sem, s).wait_send()

    @pl.loop(0, nz)
    def _(n):
        for ox in range(nx):
            e_copy(n, ox, c).wait_send()
        for ox in range(1, nx):
            d_copy(n, ox, x).wait_send()
            x_copy(n, ox).wait_send()

    @pl.loop(0, nz // 2)
    def _(p):
        for o in range(1, ny):
            y_copy(p, o).wait_send()

    @pl.loop(0, pairs)
    def _(i):
        for o in range(1, g8):
            for copy in (gx_copy, lx_copy, r_copy, v_copy):
                copy(i, o).wait_send()
        p_odd(i).wait_send()
        q_odd(i).wait_send()

        @pl.when(i < pairs - 1)
        def _():
            p_even(i).wait_send()
            q_even(i).wait_send()


def on_device(sizes, tokens, latent_grad, routes, route_weights, down_proj, expert_up, expert_down):
    nz, ny, nx, cap = sizes
    toks, depth = tokens.shape
    top = routes.shape[1]
    lat = latent_grad.shape[1]
    hid = expert_up.shape[2]
    g8, pairs, side = nx * NC, ny // 2, lat // 2
    many = 2 * cap * g8
    block = NC * nx * 2 * 16
    vmem = pl.BlockSpec(memory_space=pltpu.VMEM)
    hbm = pl.BlockSpec(memory_space=pl.ANY)
    dma = pltpu.SemaphoreType.DMA
    buffers = [
        pltpu.VMEM((toks, depth), BF),
        pltpu.VMEM((lat, hid), BF),
        pltpu.VMEM((hid, lat), BF),
        pltpu.VMEM((NC, nx, nz, ny, 16, 128), BF),
        pltpu.VMEM((block, block), BF),
        pltpu.VMEM((nz, ny // 2, block // 4, lat), BF),
        pltpu.VMEM((toks, lat), F32),
        pltpu.VMEM((2, ny, 2 * g8, toks), F32),
        pltpu.VMEM((ny, toks, lat), BF),
        pltpu.VMEM((ny, toks, lat), BF),
        pltpu.VMEM((pairs, many, 2 * toks), BF),
        pltpu.VMEM((pairs, 2 * toks, many), BF),
        pltpu.VMEM((pairs, g8, 2 * cap, lat), BF),
        pltpu.VMEM((pairs, g8, 2 * cap, lat), BF),
        pltpu.VMEM((pairs, g8, 2 * cap, lat), BF),
        pltpu.VMEM((pairs, g8, 2 * cap, lat), BF),
        pltpu.VMEM((pairs, many, hid), F32),
        pltpu.VMEM((pairs, g8, 2 * cap, lat), BF),
        pltpu.VMEM((pairs, g8, 2 * cap, lat), BF),
        pltpu.VMEM((pairs, g8, 8, 128), F32),
        pltpu.VMEM((pairs, g8, 8, 128), F32),
        pltpu.VMEM((ny, toks, lat), BF),
        pltpu.VMEM((ny, toks, lat), BF),
        pltpu.VMEM((ny, g8, toks), F32),
        pltpu.VMEM((ny, g8, toks), F32),
        pltpu.VMEM((toks, depth), BF),
        pltpu.VMEM((depth, 2 * toks), BF),
        pltpu.VMEM((toks, lat), BF),
        pltpu.VMEM((toks, side), BF),
        pltpu.VMEM((nz, nx, ny * 8, side), F32),
        pltpu.VMEM((nz, nx, ny * 8, side), BF),
        pltpu.VMEM((nx, nz, ny * 8, side), BF),
        pltpu.VMEM((nz // 2, ny, 16, side), F32),
        pltpu.VMEM((nz // 2, ny, 16, side), BF),
        pltpu.VMEM((ny, nz // 2, 16, side), BF),
        pltpu.VMEM((nz, 8, side), F32),
        pltpu.VMEM((nz, 8, side), F32),
        pltpu.VMEM((8, side), F32),
        pltpu.VMEM((8, side), F32),
    ]
    counts = [
        (ny,), (nz,), (nz, nx), (nz, nx), (ny,), (ny,), (ny,),
        (pairs, g8), (pairs, g8), (pairs, g8), (pairs, g8), (ny,), (ny,),
        (1,), (1,), (nz, nx), (nz // 2, ny), (nz,), (1,),
    ]
    input_grad, proj_grad, weight_grad = pl.pallas_call(
        functools.partial(kernel, sizes),
        out_shape=[
            jax.ShapeDtypeStruct((toks, depth), BF),
            jax.ShapeDtypeStruct((4, lat), F32),
            jax.ShapeDtypeStruct((top, toks), BF),
        ],
        in_specs=[hbm, vmem, vmem, vmem, vmem, hbm, hbm],
        out_specs=[vmem] * 3,
        scratch_shapes=buffers + [dma((3,))] + [dma((2, *count)) for count in counts],
        compiler_params=pltpu.CompilerParams(
            collective_id=0, has_side_effects=True, vmem_limit_bytes=56 * 1024 * 1024
        ),
    )(
        tokens,
        latent_grad,
        routes.T,
        route_weights.T,
        down_proj,
        expert_up[0],
        expert_down[0],
    )
    return input_grad, proj_grad, weight_grad.T


def build(mesh, nx, cap):
    nz, experts = mesh.shape["dp"], mesh.shape["expert"]
    sizes = (nz, experts // (nx * NC), nx, cap)
    both = P(("dp", "expert"), None)
    one = P("expert", None, None)
    return jax.shard_map(
        functools.partial(on_device, sizes),
        mesh=mesh,
        in_specs=(both, both, both, both, both, one, one),
        out_specs=(both, both, both),
        check_vma=False,
    )


def solution(mesh):
    return build(mesh, 4, 24)
```

time: 172 us -> 142 us (0.83)
  Pallas kernels: 165 us -> 138 us
  other arithmetic: 1.86 us -> 0 us
    pallas_call x1, Pallas kernels: 165 us -> 138 us  [on_device(): pl.pallas_call(functools.partial(kernel, sizes), out_shape=[jax.ShapeDtyp...]
    unnamed x10 -> x7, local copies, waits for them, and re-layouts: 3.83 us -> 3.15 us
where the time goes in v2:
time: 142 us
  Pallas kernels  138 us (97%)
  local copies, waits for them, and re-layouts  3.15 us (2%)
    pallas_call x1, Pallas kernels, on_device(): pl.pallas_call(functools.partial(kernel, sizes), out_shape=[jax.ShapeDtyp...  138 us
    unnamed x7, local copies, waits for them, and re-layouts  3.15 us

profile of v2, /device:TPU:1, one launch (start us, length us, event | category | flops | bytes accessed | tf_op | source)
XLA Modules:
  0.0 141.9 jit_solution(13241141703614552771)
XLA Ops:
  0.6 138.1 %shard_map.94 = (bf16[128,2048]{1,0:T(8,128)(2,1)}, f32[4,512]{1,0:T(4,128)}, bf16[8,128]{1,0:T(8,128)(2,1)}) custom-call(bf16[128,2048]{1,0:T(8,128)(2,1)} %tokens_in.1, bf16[128,512]{1,0:T(8,128)(2,1)} %grad.1, s32[8,128]{1,0:T(8,128)} %bitcast.7, bf16[8,128]{1,0:T(8,128)(2,1)} %bitcast.8, bf16[4,512]{1,0:T(4,128)(2,1)} %own_rows.1, ...), custom_call_target="tpu_custom_call" | custom-call | tf_op jit(solution)/shard_map/pallas_call | solution.py:623
  138.8 0.0 copy-start
  138.8 1.9 %copy.13 = bf16[128,2048]{1,0:T(8,128)(2,1)} copy(bf16[128,2048]{1,0:T(8,128)(2,1)} %get-tuple-element.12) | data formatting | bytes 1048576
  140.7 0.0 copy-done
  140.7 0.0 copy-start.1
  140.7 0.6 copy.14
  141.3 0.1 copy-done.1
  141.4 0.6 copy.15
Async XLA Ops:
  138.8 1.9 %copy-start = (f32[4,512]{1,0:T(4,128)S(1)}, f32[4,512]{1,0:T(4,128)}, u32[]{:S(2)}) copy-start(f32[4,512]{1,0:T(4,128)} %get-tuple-element.13) | copy-start | bytes 24580
  140.7 0.7 copy-start.1

commit v3 on v2

--- a/solution.py
+++ b/solution.py
@@ -45,15 +45,17 @@
     tokens_in, grad, routes_t, weights_t, own_rows, up_in, down_in,
     input_grad, proj_grad, weight_grad,
     tokens, up, down, units, order, proj, latent,
-    meta, g_all, l_all, pick, back, g_send, l_send, g_got, l_got, bg,
+    meta, g_all, l_all, pick, back, g_send, l_send, g_got, l_got, bg, pre_grad, grads,
     r_send, r_got, v_send, v_got, p_send, p_got, q_send, q_got,
-    tok_far, tok_t, lsum, lsum_far, pg32, pg16, x_got, s32, s16, y_got, z32, z_got, f_send, f_got,
-    sem_in, sem_b, sem_c, sem_d, sem_e, sem_m, sem_g, sem_l, sem_gx, sem_lx, sem_r, sem_v, sem_p,
-    sem_q, sem_tok, sem_ls, sem_x, sem_y, sem_z, sem_f,
+    tok_far, tok_t, lsum, lsum_far, own_sum, pg32, pg16, x_got, s32, s16, y_got, z32, z_got,
+    w32, w16, w_got, u32, u16, u_got,
+    sem_in, sem_b, sem_c, sem_d, sem_e, sem_h, sem_i, sem_j, sem_m, sem_g, sem_l, sem_gx, sem_lx, sem_r, sem_v, sem_p,
+    sem_q, sem_tok, sem_ls, sem_x, sem_y, sem_z, sem_w, sem_u,
 ):
     nz, ny, nx, cap = sizes
     g8 = nx * NC
     pairs = ny // 2
+    cut = ny * 3 // 4
     toks, depth = tokens.shape
     lat = grad.shape[1]
     hid = up.shape[1]
@@ -71,6 +73,9 @@
 
     def dev_step(d):
         return (z, (y + d + ny) % ny * g8 + me8)
+
+    def dev_cross(d):
+        return (z, (y + d + ny) % ny * g8 + xor(me8, 1, g8))
 
     def dev_8(o):
         return (z, y * g8 + xor(me8, o, g8))
@@ -84,16 +89,109 @@
     barrier = pltpu.get_barrier_semaphore()
     for o in range(1, nz):
         pl.semaphore_signal(barrier, inc=1, device_id=dev_z(o), device_id_type=MESH)
+        other = (xor(z, o, nz), y * g8 + xor(me8, 1, g8))
+        pl.semaphore_signal(barrier, inc=1, device_id=other, device_id_type=MESH)
     for o in range(1, ny):
         pl.semaphore_signal(barrier, inc=1, device_id=dev_y(o), device_id_type=MESH)
     for o in range(1, g8):
         pl.semaphore_signal(barrier, inc=1, device_id=dev_8(o), device_id_type=MESH)
+    for o in range(1, ny):
+        pl.semaphore_signal(barrier, inc=1, device_id=dev_cross(o), device_id_type=MESH)
 
     own = own_rows[...].astype(F32)
     quarters = lat // 128
     units[c, x, z, y] = jnp.concatenate(
         [own[:, 128 * k : 128 * (k + 1)] for k in range(quarters)], axis=0
     ).astype(BF)
+
+    g_all[ny - 2] = grad[...]
+    pl.semaphore_wait(barrier, 2 * (nz + ny) + g8 - 5)
+
+    sends = []
+
+    def start(cp):
+        cp.start()
+        sends.append(cp)
+
+    def b_copy(o, at_y):
+        ref = units.at[c, x, z, at_y]
+        return remote(ref, ref, sem_b, (o,), dev_y(o))
+
+    low, high = pl.ds(0, cut), pl.ds(cut, ny - cut)
+
+    def c_copy(o, at_z):
+        ref = units.at[c, x, at_z, low]
+        return remote(ref, ref, sem_c, (o,), dev_z(o))
+
+    def d_copy(o, ox, at_x):
+        ref = units.at[c, at_x, xor(z, o, nz), low]
+        return remote(ref, ref, sem_d, (o, ox), dev_8(2 * ox))
+
+    def e_copy(o, ox, at_c):
+        ref = units.at[at_c, xor(x, ox, nx), xor(z, o, nz), low]
+        return remote(ref, ref, sem_e, (o, ox), dev_8(1))
+
+    def h_copy(ox, at_x):
+        ref = units.at[c, at_x, z, high]
+        return remote(ref, ref, sem_h, (ox,), dev_8(2 * ox))
+
+    def i_copy(o, at_z):
+        ref = units.at[c, :, at_z, high]
+        return remote(ref, ref, sem_i, (o,), dev_z(o))
+
+    def j_copy(o, at_c):
+        ref = units.at[at_c, :, xor(z, o, nz), high]
+        return remote(ref, ref, sem_j, (o,), dev_8(1))
+
+    for o in range(1, ny):
+        start(b_copy(o, y))
+
+    def m_even(i):
+        return remote(
+            meta.at[0, 2 * i], meta.at[1, 2 * i + 1], sem_m, (2 * i + 1,), dev_step(i + 1)
+        )
+
+    def m_odd(i):
+        to = 2 * i + i // (pairs - 1)
+        return remote(meta.at[0, 2 * i + 1], meta.at[1, to], sem_m, (to,), dev_step(-i - 1))
+
+    def y_near(rows, sem, s):
+        away = (1, -1, 2, -2)[s]
+        return remote(rows.at[ny - 2], rows.at[s], sem, (s,), dev_step(-away))
+
+    def y_far(rows, sem, s):
+        if s < 6:
+            return remote(rows.at[s - 2], rows.at[s], sem, (s,), dev_step((-1, 1)[s - 4]))
+        at = pl.ds((7 - s) * (toks // 2), toks // 2)
+        return remote(
+            rows.at[(2, 3)[s - 6], at], rows.at[7, at], sem, (s,), dev_step((-2, 2)[s - 6])
+        )
+
+    def y_start(rows, sem):
+        for s in range(4):
+            start(y_near(rows, sem, s))
+
+    def y_wait(rows, sem, i):
+        @pl.when(i < 2)
+        def _():
+            for k in range(2):
+                @pl.when(i == k)
+                def _():
+                    y_near(rows, sem, 2 * k).wait_recv()
+                    y_near(rows, sem, 2 * k + 1).wait_recv()
+
+        @pl.when(i == 1)
+        def _():
+            for s in range(4, 8):
+                y_far(rows, sem, s).start()
+
+        for k in range(2, 4):
+            @pl.when(i == k)
+            def _():
+                y_far(rows, sem, 2 * k).wait_recv()
+                y_far(rows, sem, 2 * k + 1).wait_recv()
+
+    y_start(g_all, sem_g)
 
     row = lax.broadcasted_iota(jnp.int32, (ny * g8, toks), 0)
     slot = row // g8
@@ -117,7 +215,6 @@
         [rank.reshape(ny, g8, toks), weight.reshape(ny, g8, toks)], axis=1
     )
     meta[1, ny - 2] = meta[0, ny - 2]
-    g_all[ny - 2] = grad[...]
 
     block = NC * nx * 2 * 16
     to = lax.broadcasted_iota(jnp.int32, (block, block), 0)
@@ -128,111 +225,36 @@
     hit = origin == lax.broadcasted_iota(jnp.int32, (block, block), 1)
     order[...] = jnp.where(hit, 1.0, 0.0).astype(BF)
 
-    pl.semaphore_wait(barrier, nz + ny + g8 - 3)
-
-    sends = []
-
-    def start(cp):
-        cp.start()
-        sends.append(cp)
-
-    def b_copy(o, at_y):
-        ref = units.at[c, x, z, at_y]
-        return remote(ref, ref, sem_b, (o,), dev_y(o))
-
-    def c_copy(o, at_z):
-        ref = units.at[c, x, at_z]
-        return remote(ref, ref, sem_c, (o,), dev_z(o))
-
-    def d_copy(o, ox, at_x):
-        ref = units.at[c, at_x, xor(z, o, nz)]
-        return remote(ref, ref, sem_d, (o, ox), dev_8(2 * ox))
-
-    def e_copy(o, ox, at_c):
-        ref = units.at[at_c, xor(x, ox, nx), xor(z, o, nz)]
-        return remote(ref, ref, sem_e, (o, ox), dev_8(1))
-
-    for o in range(1, ny):
-        start(b_copy(o, y))
-
-    def m_even(i):
-        return remote(
-            meta.at[0, 2 * i], meta.at[1, 2 * i + 1], sem_m, (2 * i + 1,), dev_step(i + 1)
-        )
-
-    def m_odd(i):
-        to = 2 * i + i // (pairs - 1)
-        return remote(meta.at[0, 2 * i + 1], meta.at[1, to], sem_m, (to,), dev_step(-i - 1))
-
     for i in range(pairs):
         if i < pairs - 1:
             start(m_even(i))
         start(m_odd(i))
 
-    def y_near(rows, sem, s):
-        away = (1, -1, 2, -2)[s]
-        return remote(rows.at[ny - 2], rows.at[s], sem, (s,), dev_step(-away))
-
-    def y_far(rows, sem, s):
-        if s < 6:
-            return remote(rows.at[s - 2], rows.at[s], sem, (s,), dev_step((-1, 1)[s - 4]))
-        at = pl.ds((7 - s) * (toks // 2), toks // 2)
-        return remote(
-            rows.at[(2, 3)[s - 6], at], rows.at[7, at], sem, (s,), dev_step((-2, 2)[s - 6])
-        )
-
-    def y_start(rows, sem):
-        for s in range(4):
-            start(y_near(rows, sem, s))
-
-    def y_wait(rows, sem, i):
-        @pl.when(i < 2)
-        def _():
-            for k in range(2):
-                @pl.when(i == k)
-                def _():
-                    y_near(rows, sem, 2 * k).wait_recv()
-                    y_near(rows, sem, 2 * k + 1).wait_recv()
-
-        @pl.when(i == 1)
-        def _():
-            for s in range(4, 8):
-                y_far(rows, sem, s).start()
-
-        for k in range(2, 4):
-            @pl.when(i == k)
-            def _():
-                y_far(rows, sem, 2 * k).wait_recv()
-                y_far(rows, sem, 2 * k + 1).wait_recv()
-
-    y_start(g_all, sem_g)
+    for o in range(1, ny):
+        b_copy(o, xor(y, o, ny)).wait_recv()
+    for ox in range(1, nx):
+        start(h_copy(ox, x))
+    for o in range(1, nz):
+        start(c_copy(o, z))
+    for ox in range(1, nx):
+        h_copy(ox, xor(x, ox, nx)).wait_recv()
+    for o in range(1, nz):
+        start(i_copy(o, z))
+
+    @pl.loop(0, nz)
+    def _(o):
+        @pl.when(o > 0)
+        def _():
+            c_copy(o, xor(z, o, nz)).wait_recv()
+
+        for ox in range(1, nx):
+            d_copy(o, ox, x).start()
+        e_copy(o, 0, c).start()
+
     loads[0].wait()
     tok_copy = remote(tokens, tok_far, sem_tok, (0,), dev_8(1))
     start(tok_copy)
-
-    for o in range(1, ny):
-        b_copy(o, xor(y, o, ny)).wait_recv()
-    for o in range(1, nz):
-        start(c_copy(o, z))
-
-    @pl.loop(0, nz)
-    def _(o):
-        @pl.when(o > 0)
-        def _():
-            c_copy(o, xor(z, o, nz)).wait_recv()
-
-        for ox in range(1, nx):
-            d_copy(o, ox, x).start()
-        e_copy(o, 0, c).start()
-
-    tok_copy.wait_recv()
     tile = depth // nz
-
-    @pl.loop(0, nz)
-    def _(n):
-        at = pl.ds(pl.multiple_of(n * tile, tile), tile)
-        both = jnp.concatenate([tokens[:, at], tok_far[:, at]], axis=0)
-        tok_t[at, :] = both.astype(F32).T.astype(BF)
 
     place = lax.broadcasted_iota(jnp.int32, (cap, toks), 0).astype(F32)
 
@@ -277,10 +299,6 @@
         if i < pairs - 1:
             m_even(i).wait_recv()
         m_odd(i).wait_recv()
-    for i in range(2):
-        y_wait(g_all, sem_g, i)
-    pl.loop(0, 2)(pick_grad)
-
     latent[...] = jnp.zeros_like(latent)
 
     @pl.loop(0, nz + 1)
@@ -291,11 +309,34 @@
                 d_copy(k, ox, xor(x, ox, nx)).wait_recv()
                 e_copy(k, ox, c).start()
 
+            @pl.when(k > 0)
+            def _():
+                i_copy(k, xor(z, k, nz)).wait_recv()
+
+            j_copy(k, c).start()
+
+        @pl.when(k == nz // 4)
+        def _():
+            for i in range(2):
+                y_wait(g_all, sem_g, i)
+
+        first = nz // 4 + 1
+
+        for i in range(2, pairs):
+            @pl.when(k == first + i)
+            def _():
+                y_wait(g_all, sem_g, i)
+
+        @pl.when((k >= first) & (k < first + pairs))
+        def _():
+            pick_grad(k - first)
+
         @pl.when(k > 0)
         def _():
             o = k - 1
             for ox in range(nx):
                 e_copy(o, ox, 1 - c).wait_recv()
+            j_copy(o, 1 - c).wait_recv()
             at_z = xor(z, o, nz)
             for h in range(ny // 2):
                 mixed = units[:, :, at_z, 2 * h : 2 * h + 2].reshape(block, 128)
@@ -309,10 +350,13 @@
     l_all[ny - 2] = latent[...].astype(BF)
     y_start(l_all, sem_l)
 
-    @pl.loop(2, pairs)
-    def _(i):
-        y_wait(g_all, sem_g, i)
-        pick_grad(i)
+    tok_copy.wait_recv()
+
+    @pl.loop(0, nz)
+    def _(n):
+        at = pl.ds(pl.multiple_of(n * tile, tile), tile)
+        both = jnp.concatenate([tokens[:, at], tok_far[:, at]], axis=0)
+        tok_t[at, :] = both.astype(F32).T.astype(BF)
 
     loads[1].wait()
     loads[2].wait()
@@ -346,18 +390,22 @@
             lx_copy(i, o).wait_recv()
         rows = l_got[i].reshape(many, lat)
 
-        def unit_step(n, carry):
-            total, sums = carry
+        def unit_step(n, sums):
             at = pl.ds(pl.multiple_of(n * wide, wide), wide)
             active = jnp.maximum(dot(rows, up[:, at]), 0.0)
             part = bg[i, :, at] * active
-            sums = sums + jnp.sum(part * active, axis=1, keepdims=True)
-            return total + nt_dot((2.0 * part).astype(BF), up[:, at]), sums
-
-        total, sums = lax.fori_loop(
-            0, hid // wide, unit_step, (jnp.zeros((many, lat), F32), jnp.zeros((many, 1), F32))
-        )
-        out = total.astype(BF).reshape(g8, 2 * cap, lat)
+            pre_grad[:, at] = (2.0 * part).astype(BF)
+            part = part * active
+            for j in range(0, wide, 128):
+                sums = sums + part[:, j : j + 128]
+            return sums
+
+        sums = lax.fori_loop(0, hid // wide, unit_step, jnp.zeros((many, 128), F32))
+        sums = jnp.sum(sums, axis=1, keepdims=True)
+        for j in range(0, lat, 256):
+            rows = nt_dot(pre_grad[...], up[j : j + 256, :])
+            grads[:, j : j + 256] = rows.astype(BF)
+        out = grads[...].reshape(g8, 2 * cap, lat)
         r_got[i, 0] = out[0]
         r_send[i] = out
         for o in range(1, g8):
@@ -373,14 +421,22 @@
         for o in range(1, g8):
             v_copy(i, o).start()
 
-    def p_even(i):
+    side = lat // 2
+
+    def p_even(i, far):
+        dst = p_got.at[far, 2 * i + 1]
+        device = (dev_cross if far else dev_step)(i + 1)
+        return remote(p_send.at[far, 2 * i], dst, sem_p, (far, 2 * i + 1), device)
+
+    def p_odd(i, far):
+        to = 2 * i + i // (pairs - 1)
+        device = (dev_cross if far else dev_step)(-i - 1)
+        return remote(p_send.at[far, 2 * i + 1], p_got.at[far, to], sem_p, (far, to), device)
+
+    def p_own():
         return remote(
-            p_send.at[2 * i], p_got.at[2 * i + 1], sem_p, (2 * i + 1,), dev_step(i + 1)
+            p_send.at[1, ny - 2], p_got.at[1, ny - 2], sem_p, (1, ny - 2), dev_8(1)
         )
-
-    def p_odd(i):
-        to = 2 * i + i // (pairs - 1)
-        return remote(p_send.at[2 * i + 1], p_got.at[to], sem_p, (to,), dev_step(-i - 1))
 
     def q_even(i):
         return remote(
@@ -395,13 +451,21 @@
         for o in range(1, g8):
             r_copy(i, o).wait_recv()
         part = dot(back[i], r_got[i].reshape(many, lat)).astype(BF)
-        p_send[pl.ds(2 * i, 2)] = part.reshape(2, toks, lat)
-
-        @pl.when(i < pairs - 1)
-        def _():
-            p_even(i).start()
-
-        p_odd(i).start()
+        part = part.reshape(2, toks, lat)
+        for h in range(2):
+            far = (h + c) % 2
+            p_send[far, pl.ds(2 * i, 2)] = part[:, :, side * h : side * (h + 1)]
+        for far in range(2):
+            p_odd(i, far).start()
+
+            @pl.when(i < pairs - 1)
+            def _():
+                p_even(i, far).start()
+
+        @pl.when(i == pairs - 1)
+        def _():
+            p_own().start()
+
         for o in range(1, g8):
             v_copy(i, o).wait_recv()
         lines = []
@@ -421,12 +485,17 @@
 
         q_odd(i).start()
 
+    pl.loop(0, 2)(back_grad)
+
     @pl.loop(0, pairs + 2)
     def _(k):
         @pl.when(k < pairs)
         def _():
             dispatch(k)
-            back_grad(k)
+
+            @pl.when(k == 0)
+            def _():
+                pl.loop(2, pairs)(back_grad)
 
         @pl.when((k >= 1) & (k < pairs + 1))
         def _():
@@ -436,42 +505,60 @@
         def _():
             combine(k - 2)
 
-    total = p_send[ny - 2].astype(F32)
-    for i in range(pairs):
-        if i < pairs - 1:
-            p_even(i).wait_recv()
-            total = total + p_got[2 * i + 1].astype(F32)
-        p_odd(i).wait_recv()
-        total = total + p_got[2 * i + i // (pairs - 1)].astype(F32)
-    lsum[...] = total.astype(BF)
-    side = lat // 2
-    far_side = pl.ds(pl.multiple_of((1 - c) * side, side), side)
-    my_side = pl.ds(pl.multiple_of(c * side, side), side)
-    ls_copy = remote(lsum.at[:, far_side], lsum_far, sem_ls, (0,), dev_8(1))
+    p_own().wait_recv()
+    for far in range(2):
+        total = (p_got[1, ny - 2] if far else p_send[0, ny - 2]).astype(F32)
+        for i in range(pairs):
+            if i < pairs - 1:
+                p_even(i, far).wait_recv()
+                total = total + p_got[far, 2 * i + 1].astype(F32)
+            p_odd(i, far).wait_recv()
+            total = total + p_got[far, 2 * i + i // (pairs - 1)].astype(F32)
+        lsum[toks * far : toks * (far + 1)] = total.astype(BF)
+    ls_copy = remote(lsum.at[pl.ds(toks, toks)], lsum_far, sem_ls, (0,), dev_8(1))
     start(ls_copy)
-
-    @pl.loop(0, nz)
-    def _(n):
-        at = pl.ds(pl.multiple_of(n * tile, tile), tile)
-        input_grad[:, at] = nt_dot(lsum[...], proj[n].reshape(tile, lat)).astype(BF)
-
-    ls_copy.wait_recv()
-    pair_sum = jnp.concatenate([lsum[:, my_side], lsum_far[...]], axis=0)
 
     def x_copy(n, ox):
         src = pg16.at[n, xor(x, ox, nx)]
         return remote(src, x_got.at[ox, n], sem_x, (n, ox), dev_8(2 * ox))
 
-    @pl.loop(0, nz)
+    last = nz // 2 - 1
+    for k in range(2):
+        part = dot(tok_t[(2 * last + k) * tile : (2 * last + k + 1) * tile, :], lsum[...])
+        part = part.reshape(ny, nx * 8, side)
+        w32[:, k * nx * 8 : (k + 1) * nx * 8] = part
+        w16[:, k * nx * 8 : (k + 1) * nx * 8] = part.astype(BF)
+
+    def w_copy(o):
+        return remote(w16.at[xor(y, o, ny)], w_got.at[o], sem_w, (o,), dev_y(o))
+
+    def u_copy(ox):
+        return remote(u16.at[xor(x, ox, nx)], u_got.at[ox], sem_u, (ox,), dev_8(2 * ox))
+
+    for o in range(1, ny):
+        start(w_copy(o))
+
+    @pl.loop(0, 2 * last)
     def _(n):
         at = pl.ds(pl.multiple_of(n * tile, tile), tile)
-        part = dot(tok_t[at, :], pair_sum).reshape(ny, nx, 8, side)
+        part = dot(tok_t[at, :], lsum[...]).reshape(ny, nx, 8, side)
         for k in range(nx):
             piece = part[:, k].reshape(ny * 8, side)
             pg32[n, k] = piece
             pg16[n, k] = piece.astype(BF)
         for ox in range(1, nx):
             x_copy(n, ox).start()
+
+    ls_copy.wait_recv()
+    near, other = lsum[:toks], lsum_far[...]
+    own_sum[...] = jnp.concatenate(
+        [jnp.where(c == 0, near, other), jnp.where(c == 0, other, near)], axis=1
+    )
+
+    @pl.loop(0, nz)
+    def _(n):
+        at = pl.ds(pl.multiple_of(n * tile, tile), tile)
+        input_grad[:, at] = nt_dot(own_sum[...], proj[n].reshape(tile, lat)).astype(BF)
 
     for i in range(pairs):
         if i < pairs - 1:
@@ -489,8 +576,7 @@
         src = s16.at[p, xor(y, o, ny)]
         return remote(src, y_got.at[o, p], sem_y, (p, o), dev_y(o))
 
-    @pl.loop(0, nz // 2)
-    def _(p):
+    def x_sum(p):
         halves = []
         for s in range(2):
             n = 2 * p + s
@@ -505,7 +591,22 @@
         for o in range(1, ny):
             y_copy(p, o).start()
 
-    @pl.loop(0, nz // 2)
+    early = min(2, last)
+    pl.loop(0, early)(x_sum)
+    total = w32[y]
+    for o in range(1, ny):
+        w_copy(o).wait_recv()
+        total = total + w_got[o].astype(F32)
+    total = total.reshape(2, nx, 8, side)
+    for k in range(nx):
+        piece = total[:, k].reshape(16, side)
+        u32[k] = piece
+        u16[k] = piece.astype(BF)
+    for ox in range(1, nx):
+        start(u_copy(ox))
+    pl.loop(early, last)(x_sum)
+
+    @pl.loop(0, last)
     def _(p):
         total = s32[p, y]
         for o in range(1, ny):
@@ -513,21 +614,32 @@
             total = total + y_got[o, p].astype(F32)
         z32[pl.ds(2 * p, 2)] = total.reshape(2, 8, side)
 
-    def z_copy(o):
-        return remote(z32.at[xor(z, o, nz)], z_got.at[o], sem_z, (o,), dev_z(o))
-
-    for o in range(1, nz):
-        start(z_copy(o))
+    total = u32[x]
+    for ox in range(1, nx):
+        u_copy(ox).wait_recv()
+        total = total + u_got[ox].astype(F32)
+    z32[2 * last : 2 * last + 2] = total.reshape(2, 8, side)
+
+    def z_copy(o, far):
+        device = (xor(z, o, nz), y * g8 + xor(me8, far, g8))
+        return remote(z32.at[xor(z, o, nz)], z_got.at[far, o], sem_z, (far, o), device)
+
+    for o in range(nz):
+        for far in range(0 if o else 1, 2):
+            start(z_copy(o, far))
+    far_side = pl.ds(pl.multiple_of((1 - c) * side, side), side)
+    my_side = pl.ds(pl.multiple_of(c * side, side), side)
     total = z32[z]
     for o in range(1, nz):
-        z_copy(o).wait_recv()
-        total = total + z_got[o]
-    f_send[...] = total
-    f_copy = remote(f_send, f_got, sem_f, (0,), dev_8(1))
-    start(f_copy)
+        z_copy(o, 0).wait_recv()
+        total = total + z_got[0, o]
     proj_grad[:, my_side] = jnp.where(c == 0, total[:4], total[4:])
-    f_copy.wait_recv()
-    proj_grad[:, far_side] = jnp.where(c == 0, f_got[:4, :], f_got[4:, :])
+    z_copy(0, 1).wait_recv()
+    total = z_got[1, 0]
+    for o in range(1, nz):
+        z_copy(o, 1).wait_recv()
+        total = total + z_got[1, o]
+    proj_grad[:, far_side] = jnp.where(c == 0, total[:4], total[4:])
 
     for cp in sends:
         cp.wait_send()
@@ -535,15 +647,22 @@
         for s in range(4, 8):
             y_far(rows, sem, s).wait_send()
 
+    p_own().wait_send()
+
     @pl.loop(0, nz)
     def _(n):
+        j_copy(n, c).wait_send()
         for ox in range(nx):
             e_copy(n, ox, c).wait_send()
         for ox in range(1, nx):
             d_copy(n, ox, x).wait_send()
+
+    @pl.loop(0, 2 * last)
+    def _(n):
+        for ox in range(1, nx):
             x_copy(n, ox).wait_send()
 
-    @pl.loop(0, nz // 2)
+    @pl.loop(0, last)
     def _(p):
         for o in range(1, ny):
             y_copy(p, o).wait_send()
@@ -553,13 +672,15 @@
         for o in range(1, g8):
             for copy in (gx_copy, lx_copy, r_copy, v_copy):
                 copy(i, o).wait_send()
-        p_odd(i).wait_send()
         q_odd(i).wait_send()
+        for far in range(2):
+            p_odd(i, far).wait_send()
 
         @pl.when(i < pairs - 1)
         def _():
-            p_even(i).wait_send()
             q_even(i).wait_send()
+            for far in range(2):
+                p_even(i, far).wait_send()
 
 
 def on_device(sizes, tokens, latent_grad, routes, route_weights, down_proj, expert_up, expert_down):
@@ -592,18 +713,21 @@
         pltpu.VMEM((pairs, g8, 2 * cap, lat), BF),
         pltpu.VMEM((pairs, g8, 2 * cap, lat), BF),
         pltpu.VMEM((pairs, many, hid), F32),
+        pltpu.VMEM((many, hid), BF),
+        pltpu.VMEM((many, lat), BF),
         pltpu.VMEM((pairs, g8, 2 * cap, lat), BF),
         pltpu.VMEM((pairs, g8, 2 * cap, lat), BF),
         pltpu.VMEM((pairs, g8, 8, 128), F32),
         pltpu.VMEM((pairs, g8, 8, 128), F32),
-        pltpu.VMEM((ny, toks, lat), BF),
-        pltpu.VMEM((ny, toks, lat), BF),
+        pltpu.VMEM((2, ny, toks, side), BF),
+        pltpu.VMEM((2, ny, toks, side), BF),
         pltpu.VMEM((ny, g8, toks), F32),
         pltpu.VMEM((ny, g8, toks), F32),
         pltpu.VMEM((toks, depth), BF),
         pltpu.VMEM((depth, 2 * toks), BF),
+        pltpu.VMEM((2 * toks, side), BF),
+        pltpu.VMEM((toks, side), BF),
         pltpu.VMEM((toks, lat), BF),
-        pltpu.VMEM((toks, side), BF),
         pltpu.VMEM((nz, nx, ny * 8, side), F32),
         pltpu.VMEM((nz, nx, ny * 8, side), BF),
         pltpu.VMEM((nx, nz, ny * 8, side), BF),
@@ -611,14 +735,18 @@
         pltpu.VMEM((nz // 2, ny, 16, side), BF),
         pltpu.VMEM((ny, nz // 2, 16, side), BF),
         pltpu.VMEM((nz, 8, side), F32),
-        pltpu.VMEM((nz, 8, side), F32),
-        pltpu.VMEM((8, side), F32),
-        pltpu.VMEM((8, side), F32),
+        pltpu.VMEM((2, nz, 8, side), F32),
+        pltpu.VMEM((ny, 2 * nx * 8, side), F32),
+        pltpu.VMEM((ny, 2 * nx * 8, side), BF),
+        pltpu.VMEM((ny, 2 * nx * 8, side), BF),
+        pltpu.VMEM((nx, 16, side), F32),
+        pltpu.VMEM((nx, 16, side), BF),
+        pltpu.VMEM((nx, 16, side), BF),
     ]
     counts = [
-        (ny,), (nz,), (nz, nx), (nz, nx), (ny,), (ny,), (ny,),
-        (pairs, g8), (pairs, g8), (pairs, g8), (pairs, g8), (ny,), (ny,),
-        (1,), (1,), (nz, nx), (nz // 2, ny), (nz,), (1,),
+        (ny,), (nz,), (nz, nx), (nz, nx), (nx,), (nz,), (nz,), (ny,), (ny,), (ny,),
+        (pairs, g8), (pairs, g8), (pairs, g8), (pairs, g8), (2, ny), (ny,),
+        (1,), (1,), (nz, nx), (nz // 2, ny), (2, nz), (ny,), (nx,),
     ]
     input_grad, proj_grad, weight_grad = pl.pallas_call(
         functools.partial(kernel, sizes),

time: 142 us -> 136 us (0.958)
  Pallas kernels: 138 us -> 132 us
    pallas_call x1, Pallas kernels: 138 us -> 132 us  [on_device(): pl.pallas_call(functools.partial(kernel, sizes), out_shape=[jax.ShapeDtyp...]
where the time goes in v3:
time: 136 us; the launch traced here: 135 us
  Pallas kernels  132 us (97%)
  local copies, waits for them, and re-layouts  3.15 us (2%)
    pallas_call x1, Pallas kernels, on_device(): pl.pallas_call(functools.partial(kernel, sizes), out_shape=[jax.ShapeDtyp...  132 us
    unnamed x7, local copies, waits for them, and re-layouts  3.15 us

profile of v3, /device:TPU:1, one launch (start us, length us, event | category | flops | bytes accessed | tf_op | source)
XLA Modules:
  0.0 135.3 jit_solution(4141299669929868516)
XLA Ops:
  0.6 131.5 %shard_map.94 = (bf16[128,2048]{1,0:T(8,128)(2,1)}, f32[4,512]{1,0:T(4,128)}, bf16[8,128]{1,0:T(8,128)(2,1)}) custom-call(bf16[128,2048]{1,0:T(8,128)(2,1)} %tokens_in.1, bf16[128,512]{1,0:T(8,128)(2,1)} %grad.1, s32[8,128]{1,0:T(8,128)} %bitcast.7, bf16[8,128]{1,0:T(8,128)(2,1)} %bitcast.8, bf16[4,512]{1,0:T(4,128)(2,1)} %own_rows.1, ...), custom_call_target="tpu_custom_call" | custom-call | tf_op jit(solution)/shard_map/pallas_call | solution.py:751
  132.2 0.0 copy-start
  132.2 1.9 %copy.13 = bf16[128,2048]{1,0:T(8,128)(2,1)} copy(bf16[128,2048]{1,0:T(8,128)(2,1)} %get-tuple-element.12) | data formatting | bytes 1048576
  134.1 0.0 copy-done
  134.1 0.0 copy-start.1
  134.1 0.6 copy.14
  134.7 0.1 copy-done.1
  134.7 0.6 copy.15
Async XLA Ops:
  132.2 1.9 %copy-start = (f32[4,512]{1,0:T(4,128)S(1)}, f32[4,512]{1,0:T(4,128)}, u32[]{:S(2)}) copy-start(f32[4,512]{1,0:T(4,128)} %get-tuple-element.13) | copy-start | bytes 24580
  134.1 0.7 copy-start.1

commit v4 on v3

--- a/solution.py
+++ b/solution.py
@@ -382,8 +382,8 @@
     def r_copy(i, o):
         return remote(r_send.at[i, o], r_got.at[i, o], sem_r, (i, o), dev_8(o))
 
-    def v_copy(i, o):
-        return remote(v_send.at[i, o], v_got.at[i, o], sem_v, (i, o), dev_8(o))
+    def v_copy(o):
+        return remote(v_send.at[o], v_got.at[o], sem_v, (o,), dev_8(o))
 
     def experts(i):
         for o in range(1, g8):
@@ -413,13 +413,12 @@
         for o in range(g8):
             column = sums[2 * cap * o : 2 * cap * (o + 1)]
             line = jnp.sum(jnp.where(lane_is_row, column, 0.0), axis=0, keepdims=True)
-            line = jnp.broadcast_to(line, (8, 128))
-            if o == 0:
-                v_got[i, 0] = line
-            else:
-                v_send[i, o] = line
-        for o in range(1, g8):
-            v_copy(i, o).start()
+            v_send[o, pl.ds(i, 1), :] = line
+
+        @pl.when(i == pairs - 1)
+        def _():
+            for o in range(1, g8):
+                v_copy(o).start()
 
     side = lat // 2
 
@@ -466,12 +465,37 @@
         def _():
             p_own().start()
 
-        for o in range(1, g8):
-            v_copy(i, o).wait_recv()
+    v_send[...] = jnp.zeros_like(v_send)
+    pl.loop(0, 2)(back_grad)
+
+    @pl.loop(0, pairs + 2)
+    def _(k):
+        @pl.when(k < pairs)
+        def _():
+            dispatch(k)
+
+            @pl.when(k == 0)
+            def _():
+                pl.loop(2, pairs)(back_grad)
+
+        @pl.when((k >= 1) & (k < pairs + 1))
+        def _():
+            experts(k - 1)
+
+        @pl.when(k >= 2)
+        def _():
+            combine(k - 2)
+
+    v_got[0] = v_send[0]
+    for o in range(1, g8):
+        v_copy(o).wait_recv()
+
+    @pl.loop(0, pairs)
+    def _(i):
         lines = []
         for o in range(g8):
             column = jnp.sum(
-                jnp.where(lane_is_row, v_got[i, o, 0:1, :], 0.0), axis=1, keepdims=True
+                jnp.where(lane_is_row, v_got[o, pl.ds(i, 1), :], 0.0), axis=1, keepdims=True
             )
             block = pick[i, 2 * cap * o : 2 * cap * (o + 1), :].astype(F32)
             lines.append(jnp.sum(block * column, axis=0, keepdims=True))
@@ -484,26 +508,6 @@
             q_even(i).start()
 
         q_odd(i).start()
-
-    pl.loop(0, 2)(back_grad)
-
-    @pl.loop(0, pairs + 2)
-    def _(k):
-        @pl.when(k < pairs)
-        def _():
-            dispatch(k)
-
-            @pl.when(k == 0)
-            def _():
-                pl.loop(2, pairs)(back_grad)
-
-        @pl.when((k >= 1) & (k < pairs + 1))
-        def _():
-            experts(k - 1)
-
-        @pl.when(k >= 2)
-        def _():
-            combine(k - 2)
 
     p_own().wait_recv()
     for far in range(2):
@@ -648,6 +652,8 @@
             y_far(rows, sem, s).wait_send()
 
     p_own().wait_send()
+    for o in range(1, g8):
+        v_copy(o).wait_send()
 
     @pl.loop(0, nz)
     def _(n):
@@ -670,7 +676,7 @@
     @pl.loop(0, pairs)
     def _(i):
         for o in range(1, g8):
-            for copy in (gx_copy, lx_copy, r_copy, v_copy):
+            for copy in (gx_copy, lx_copy, r_copy):
                 copy(i, o).wait_send()
         q_odd(i).wait_send()
         for far in range(2):
@@ -717,8 +723,8 @@
         pltpu.VMEM((many, lat), BF),
         pltpu.VMEM((pairs, g8, 2 * cap, lat), BF),
         pltpu.VMEM((pairs, g8, 2 * cap, lat), BF),
-        pltpu.VMEM((pairs, g8, 8, 128), F32),
-        pltpu.VMEM((pairs, g8, 8, 128), F32),
+        pltpu.VMEM((g8, 8, 128), F32),
+        pltpu.VMEM((g8, 8, 128), F32),
         pltpu.VMEM((2, ny, toks, side), BF),
         pltpu.VMEM((2, ny, toks, side), BF),
         pltpu.VMEM((ny, g8, toks), F32),
@@ -745,7 +751,7 @@
     ]
     counts = [
         (ny,), (nz,), (nz, nx), (nz, nx), (nx,), (nz,), (nz,), (ny,), (ny,), (ny,),
-        (pairs, g8), (pairs, g8), (pairs, g8), (pairs, g8), (2, ny), (ny,),
+        (pairs, g8), (pairs, g8), (pairs, g8), (g8,), (2, ny), (ny,),
         (1,), (1,), (nz, nx), (nz // 2, ny), (2, nz), (ny,), (nx,),
     ]
     input_grad, proj_grad, weight_grad = pl.pallas_call(

time: 136 us -> 134 us (0.985)
  Pallas kernels: 132 us -> 130 us
where the time goes in v4:
time: 134 us
  Pallas kernels  130 us (97%)
  local copies, waits for them, and re-layouts  3.15 us (2%)
    pallas_call x1, Pallas kernels, on_device(): pl.pallas_call(functools.partial(kernel, sizes), out_shape=[jax.ShapeDtyp...  130 us
    unnamed x7, local copies, waits for them, and re-layouts  3.15 us

profile of v4, /device:TPU:1, one launch (start us, length us, event | category | flops | bytes accessed | tf_op | source)
XLA Modules:
  0.0 134.1 jit_solution(11073687119664727660)
XLA Ops:
  0.6 130.3 %shard_map.94 = (bf16[128,2048]{1,0:T(8,128)(2,1)}, f32[4,512]{1,0:T(4,128)}, bf16[8,128]{1,0:T(8,128)(2,1)}) custom-call(bf16[128,2048]{1,0:T(8,128)(2,1)} %tokens_in.1, bf16[128,512]{1,0:T(8,128)(2,1)} %grad.1, s32[8,128]{1,0:T(8,128)} %bitcast.7, bf16[8,128]{1,0:T(8,128)(2,1)} %bitcast.8, bf16[4,512]{1,0:T(4,128)(2,1)} %own_rows.1, ...), custom_call_target="tpu_custom_call" | custom-call | tf_op jit(solution)/shard_map/pallas_call | solution.py:757
  130.9 0.0 copy-start
  130.9 1.9 %copy.13 = bf16[128,2048]{1,0:T(8,128)(2,1)} copy(bf16[128,2048]{1,0:T(8,128)(2,1)} %get-tuple-element.12) | data formatting | bytes 1048576
  132.8 0.0 copy-done
  132.8 0.0 copy-start.1
  132.8 0.6 copy.14
  133.4 0.1 copy-done.1
  133.5 0.6 copy.15
Async XLA Ops:
  130.9 1.9 %copy-start = (f32[4,512]{1,0:T(4,128)S(1)}, f32[4,512]{1,0:T(4,128)}, u32[]{:S(2)}) copy-start(f32[4,512]{1,0:T(4,128)} %get-tuple-element.13) | copy-start | bytes 24580
  132.8 0.7 copy-start.1
